TPU v7x, 32 devices: a whole 2x2x4 slice. The times are simulated.
32 devices in a mesh: blk: 8 (over y, x, core), grp: 4 (over z).
Axes of the slice: x: 2, y: 2, z: 4, core: 2. Of those that a mesh axis runs over, the one named last changes fastest.
Arguments:
- a_tiles: bfloat16 [256, 64, 1024], P(('blk', 'grp')), may hold values from -0.75 to 0.75
- a_cols: int32 [256, 16], P(('blk', 'grp')), may hold values from 0 to 255, as said below
- p_tiles: bfloat16 [256, 64, 256], P(('blk', 'grp')), may hold values from -0.75 to 0.75
- route_list: int32 [256, 256], P(('blk', 'grp')), may hold values from 0 to 255, as said below
- out_slot: int32 [32, 256], P(('blk', 'grp')), may hold values from 0 to 127, as said below
Outputs:
- coarse_blocks: float32 [4096, 4096], P(('blk', 'grp'))
Inputs may be any that keep to these rules, and one draw needn't show every extreme that they name: `a_cols`: fine block row f is held by device f // 8 of blk+grp. Every entry in the rows of one device names a fine block row held by a device with the same grp index, and among the 128 entries of one device's rows exactly 16 name rows held by each blk index. `route_list`: A value o * 64 + p sends the partial block to send position p for the device with grp index o and the same blk index. For each device and each o, no position at or above a count is used, the count being at least 16, and 64 for one o of each device. `out_slot`: entry o * 64 + p of row d is the output block, among the 128 of the device with grp index o and the blk index of device d, into which send position p of device d adds; each output block index stands exactly 4 * 64 // 128 times in a row.
All inputs are finite; a program needn't handle non-finite values.
Results may differ from a plain program's by a relative error of at most 0.0029.
Values may be sent and summed in bfloat16 or wider, within the bound.
No kernel may reach another device: no remote copies, remote signals or barrier semaphores. Data moves between devices by JAX's collectives and lax.ppermute only.
A program may use at most 128 MiB of HBM per device.

v0:
```python
import functools

import jax
import jax.numpy as jnp
from jax import lax
from jax.experimental import pallas as pl
from jax.experimental.pallas import tpu as pltpu
from jax.sharding import PartitionSpec as P

OSLOT = 128
LANES = 128
ACCS = 4
AHEAD = 2
NAME_ROWS = 16
PART = 256
PARTS = 2


def log2(n):
    assert n & (n - 1) == 0
    return n.bit_length() - 1


def number_columns(n_places):
    return 0, n_places, 2 * n_places, 2 * n_places + LANES


def numbers_kernel(a_ref, route_ref, slot_ref, cols_ref, out_ref, wide):
    rf, tile, width = a_ref.shape
    out_ref[:rf * tile, :] = a_ref[...].reshape(rf * tile, width)
    wide[...] = jnp.zeros_like(wide)
    cols = cols_ref[...]
    parts = (route_ref[...], slot_ref[...], lax.shift_right_logical(cols, jnp.int32(log2(PART))), cols & (PART - 1))
    for at, part in zip(number_columns(route_ref.shape[1]), parts):
        wide[:part.shape[0], at:at + part.shape[1]] = part.astype(jnp.float32)
    out_ref[rf * tile:, :] = wide[...].astype(out_ref.dtype)


def with_numbers(a_tiles, route_list, out_slot, a_cols):
    rf, tile, width = a_tiles.shape
    return pl.pallas_call(
        numbers_kernel,
        out_shape=jax.ShapeDtypeStruct((rf * tile + NAME_ROWS, width), a_tiles.dtype),
        scratch_shapes=[pltpu.VMEM((NAME_ROWS, width), jnp.float32)],
        compiler_params=pltpu.CompilerParams(vmem_limit_bytes=56 * 1024 * 1024),
        cost_estimate=pl.CostEstimate(flops=1, bytes_accessed=1, transcendentals=0),
        name="with_numbers",
    )(a_tiles, route_list, out_slot, a_cols)


def partial_kernel(n_pieces, spans, cap, groups, table_of, rows_in, *refs):
    pieces, refs = refs[:n_pieces], refs[n_pieces:]
    outs, refs = refs[:len(spans)], refs[len(spans):]
    accs, (a_ref, lhs_ref, panel, y_buf, w_buf, *rest, sems) = refs[:ACCS], refs[ACCS:]
    packed_ref, place_vmem, idx_vmem, place_ref, idx_ref = rest
    tile = panel.shape[1]
    rf, tiles = a_ref.shape[0] // tile, a_ref.shape[1] // tile
    width = panel.shape[2] // tile
    sub = tile * tile // LANES
    n_tables = accs[0].shape[0] // cap
    chunk = 8

    n_places = width * tiles * width
    copies = [
        pltpu.make_async_copy(rows_in.at[pl.ds(rf * tile, NAME_ROWS)], packed_ref, sems.at[0]),
    ]
    for n in range(0, rf, PARTS):
        part = pl.ds(n * tile, PARTS * tile)
        copies.append(pltpu.make_async_copy(rows_in.at[part], a_ref.at[part], sems.at[len(copies)]))
    at = 0
    for piece in pieces:
        for n in range(0, piece.shape[0], rf):
            part, whole = piece.at[pl.ds(n, rf)], panel.at[pl.ds(at, rf)]
            copies.append(pltpu.make_async_copy(part, whole, sems.at[len(copies)]))
            at += rf
    for copy in copies:
        copy.start()
    copies.pop(0).wait()

    me, blk = lax.axis_index("grp"), lax.axis_index("blk")
    numbers = packed_ref[...].astype(jnp.float32).astype(jnp.int32)
    at_route, at_slot, at_high, at_low = number_columns(n_places)
    route = numbers[:rf, at_route:at_route + n_places]
    names = numbers[:1, at_slot:at_slot + n_places].astype(jnp.float32)
    owner = lax.shift_right_logical(route, jnp.int32(log2(cap)))
    table = table_of(owner ^ me, (me == 1) | (me == 2))
    place_vmem[...] = jnp.where(table < n_tables, table * cap + (route & (cap - 1)), n_tables * cap)
    cols = numbers[:rf, at_high:at_high + LANES] * PART + numbers[:rf, at_low:at_low + LANES]
    d = lax.shift_right_logical(cols, jnp.int32(log2(rf * groups))) ^ blk
    half = panel.shape[0] // (2 * rf)
    idx_vmem[...] = ((d & 1) * half + lax.shift_right_logical(d, jnp.int32(1))) * rf + (cols & (rf - 1))
    for n, (src, dst) in enumerate(((place_vmem, place_ref), (idx_vmem, idx_ref))):
        copy = pltpu.make_async_copy(src, dst, sems.at[sems.shape[0] - 2 + n])
        copy.start()
        copies.append(copy)

    def clear(c, carry):
        blocks = pl.ds(c * chunk, chunk)
        for acc in accs:
            acc[blocks] = jnp.zeros((chunk, sub, LANES), jnp.float32)
        return carry

    lax.fori_loop(0, n_tables * cap // chunk, clear, 0)
    for acc in accs:
        acc[n_tables * cap] = jnp.zeros((sub, LANES), jnp.float32)
    for copy in copies:
        copy.wait()

    columns = width * tile
    from_col = lax.broadcasted_iota(jnp.int32, (columns, columns), 0)
    to_col = lax.broadcasted_iota(jnp.int32, (columns, columns), 1)
    wanted = jnp.where(to_col < columns // 2, 2 * to_col, 2 * to_col - columns + 1)
    chosen = jnp.where(from_col == wanted, 1.0, 0.0).astype(jnp.bfloat16)
    for row in range(rf):
        split = jnp.dot(panel[row], chosen, preferred_element_type=jnp.float32)
        stacked = jnp.concatenate([split[:, :columns // 2], split[:, columns // 2:]], axis=0)
        lhs_ref[row] = jnp.transpose(stacked).astype(jnp.bfloat16)

    lane = lax.broadcasted_iota(jnp.int32, (tile, LANES), 1)
    lo = lane < tile

    def first_products(row, k):
        both = a_ref[pl.ds(pl.multiple_of(row * tile, tile), tile), k * tile:k * tile + LANES]
        none = jnp.zeros_like(both)
        left = jnp.concatenate([jnp.where(lo, both, none), jnp.where(lo, none, both)], axis=0)
        right = jnp.concatenate([panel[idx_ref[row, k]], panel[idx_ref[row, k + 1]]], axis=0)
        return jnp.dot(left, right, preferred_element_type=jnp.float32)

    def keep(u, y):
        for m in range(width // 2):
            x = y[:, m * LANES:(m + 1) * LANES]
            y_buf[u, :, 2 * m * LANES:(2 * m + 1) * LANES] = x.astype(jnp.bfloat16)
            y_buf[u, :, (2 * m + 1) * LANES:(2 * m + 2) * LANES] = pltpu.roll(x, tile, 1).astype(jnp.bfloat16)

    def second_product(row, u):
        lhs = lhs_ref[row]
        w = []
        for m in range(width // 2):
            x = y_buf[u, :, 2 * m * LANES:(2 * m + 1) * LANES]
            xr = y_buf[u, :, (2 * m + 1) * LANES:(2 * m + 2) * LANES]
            none = jnp.zeros_like(x)
            right = jnp.concatenate(
                [
                    jnp.concatenate([jnp.where(lo, x, none), jnp.where(lo, xr, none)], axis=1),
                    jnp.concatenate([jnp.where(lo, none, xr), jnp.where(lo, none, x)], axis=1),
                ],
                axis=0,
            )
            w.append(jnp.dot(lhs, right, preferred_element_type=jnp.float32))
        return w

    def add(row, k, w):
        for q in range(width):
            part = w[q // 2][:, q % 2 * LANES:(q % 2 + 1) * LANES]
            for s in range(0, width, ACCS):
                group = range(s, min(s + ACCS, width))
                places = [place_ref[row, (n * tiles + k) * width + q] for n in group]
                old = [acc[place] for acc, place in zip(accs, places)]
                for acc, place, was, n in zip(accs, places, old, group):
                    acc[place] = was + part[n * sub:(n + 1) * sub]

    def keep_two(u, y):
        keep(u, y[:tile])
        keep(u + 1, y[tile:])

    def hold(n, w):
        for m, part in enumerate(w):
            w_buf[n, :, m * 2 * LANES:(m + 1) * 2 * LANES] = part

    def held(n):
        return [w_buf[n, :, m * 2 * LANES:(m + 1) * 2 * LANES] for m in range(width // 2)]

    for k in range(0, tiles, 2):
        keep_two(k, first_products(0, k))
    for n in range(AHEAD):
        hold(n, second_product(0, n))

    def block_row(row, carry):
        following = jnp.minimum(row + 1, rf - 1)
        w = [held(n) for n in range(AHEAD)]
        for k in range(tiles):
            if k % 2 == 0:
                upcoming = first_products(following, k)
            ahead = k + AHEAD
            w.append(second_product(row, ahead) if ahead < tiles else second_product(following, ahead - tiles))
            add(row, k, w.pop(0))
            if k % 2 == 1:
                keep_two(k - 1, upcoming)
        for n in range(AHEAD):
            hold(n, w[n])
        return carry

    lax.fori_loop(0, rf, block_row, 0)

    named = jnp.zeros((NAME_ROWS, LANES), jnp.float32)
    here = lax.broadcasted_iota(jnp.int32, named.shape, 0)
    for n in range(groups * cap // LANES):
        part = names[:, n * LANES:(n + 1) * LANES]
        named = jnp.where(here == n, jnp.broadcast_to(part, named.shape), named)

    for (first, count), out in zip(spans, outs):

        def merge(c, carry):
            blocks = pl.ds(first + c * chunk, chunk)
            total = accs[0][blocks]
            for acc in accs[1:]:
                total = total + acc[blocks]
            rows = pl.ds(pl.multiple_of(c * (chunk * sub), chunk * sub), chunk * sub)
            out[rows, :] = total.reshape(chunk * sub, LANES).astype(out.dtype)
            return carry

        lax.fori_loop(0, count // chunk, merge, 0)
        out[count * sub:, :] = named.astype(out.dtype)


def partial_sums(rows_in, pieces, table_of, tables, spans, groups, cap):
    tile, cols = pieces[0].shape[1], rows_in.shape[1]
    rf = (rows_in.shape[0] - NAME_ROWS) // tile
    sub = tile * tile // LANES
    width = pieces[0].shape[2]
    rows = sum(x.shape[0] for x in pieces)
    n_places = (width // tile) ** 2 * (cols // tile)
    operands = [rows_in] + pieces
    panel_bytes = rows * tile * width * 2
    return pl.pallas_call(
        functools.partial(partial_kernel, len(pieces), spans, cap, groups, table_of),
        out_shape=[jax.ShapeDtypeStruct((n * sub + NAME_ROWS, LANES), jnp.bfloat16) for _, n in spans],
        grid_spec=pl.GridSpec(
            grid=(1,),
            in_specs=[pl.BlockSpec(memory_space=pl.ANY)] * len(operands),
            out_specs=[pl.BlockSpec((n * sub + NAME_ROWS, LANES), lambda i: (0, 0)) for _, n in spans],
            scratch_shapes=[pltpu.VMEM((tables * cap + 1, sub, LANES), jnp.float32)] * ACCS
            + [
                pltpu.VMEM((rf * tile, cols), jnp.bfloat16),
                pltpu.VMEM((rf, width // 2, 2 * tile), jnp.bfloat16),
                pltpu.VMEM((rows, tile, width), jnp.bfloat16),
                pltpu.VMEM((cols // tile, tile, 2 * width), jnp.bfloat16),
                pltpu.VMEM((AHEAD, width // 2, 2 * width), jnp.float32),
                pltpu.VMEM((NAME_ROWS, cols), jnp.bfloat16),
                pltpu.VMEM((rf, n_places), jnp.int32),
                pltpu.VMEM((rf, LANES), jnp.int32),
                pltpu.SMEM((rf, n_places), jnp.int32),
                pltpu.SMEM((rf, LANES), jnp.int32),
                pltpu.SemaphoreType.DMA((3 + rf // PARTS + rows // rf,)),
            ],
        ),
        compiler_params=pltpu.CompilerParams(
            dimension_semantics=("arbitrary",), vmem_limit_bytes=26 * 1024 * 1024 + panel_bytes
        ),
        cost_estimate=pl.CostEstimate(flops=1, bytes_accessed=1, transcendentals=0),
        name="partial_sums",
    )(*operands)


def early_kernel(*refs):
    tables, out_ref, accs, (vmem_names, smem_names, sem) = refs[:3], refs[3], refs[4:-3], refs[-3:]
    n_out, sub = out_ref.shape[:2]
    cap = (tables[0].shape[0] - NAME_ROWS) // sub
    chunk = 8
    at = lax.axis_index("grp") * cap
    row, lane = lax.div(at, jnp.int32(LANES)), lax.rem(at, jnp.int32(LANES))

    for n, x in enumerate(tables):
        vmem_names[n] = x[pl.ds(cap * sub, NAME_ROWS), :].astype(jnp.float32).astype(jnp.int32)
    copy = pltpu.make_async_copy(vmem_names, smem_names, sem)
    copy.start()

    def clear(c, carry):
        for acc in accs:
            acc[pl.ds(c * chunk, chunk)] = jnp.zeros((chunk, sub, LANES), jnp.float32)
        return carry

    lax.fori_loop(0, n_out // chunk, clear, 0)
    copy.wait()

    def add(c, carry):
        src = pl.ds(pl.multiple_of(c * sub, sub), sub)
        names = [smem_names[n, row, lane + c] for n in range(len(tables))]
        old = [acc[name] for acc, name in zip(accs, names)]
        for acc, name, was, x in zip(accs, names, old, tables):
            acc[name] = was + x[src, :].astype(jnp.float32)
        return carry

    lax.fori_loop(0, cap, add, 0, unroll=4)

    def merge(c, carry):
        blocks = pl.ds(c * chunk, chunk)
        total = accs[0][blocks]
        for acc in accs[1:]:
            total = total + acc[blocks]
        out_ref[blocks] = total
        return carry

    lax.fori_loop(0, n_out // chunk, merge, 0)


def last_kernel(table, from_b, from_c, out_ref, acc, late, rows_buf, vmem_names, smem_names, sems):
    n_out, sub = acc.shape[:2]
    cap = (late.shape[0] - NAME_ROWS) // sub
    me = lax.axis_index("grp")
    at = me * cap
    row, lane = lax.div(at, jnp.int32(LANES)), lax.rem(at, jnp.int32(LANES))
    parts = (sems.shape[0] - 2) // 3

    def late_copies(table_in):
        spans = [pl.ds(cap * sub, NAME_ROWS)]
        spans += [pl.ds(n * (cap // parts) * sub, cap // parts * sub) for n in range(parts)]
        return [
            pltpu.make_async_copy(table_in.at[span], late.at[span], sems.at[n]) for n, span in enumerate(spans)
        ]

    middle = (me == 1) | (me == 2)

    @pl.when(middle)
    def _():
        for copy in late_copies(from_b):
            copy.start()

    @pl.when(jnp.logical_not(middle))
    def _():
        for copy in late_copies(from_c):
            copy.start()

    height = n_out // parts
    blocks = [pl.ds(n * height, height) for n in range(parts)]
    fills = [
        pltpu.make_async_copy(table.at[span], acc.at[span], sems.at[1 + parts + n]) for n, span in enumerate(blocks)
    ]
    for copy in fills:
        copy.start()
    waiting = late_copies(from_b)
    waiting.pop(0).wait()
    vmem_names[...] = late[pl.ds(cap * sub, NAME_ROWS), :].astype(jnp.float32).astype(jnp.int32)
    copy = pltpu.make_async_copy(vmem_names, smem_names, sems.at[1 + 2 * parts])
    copy.start()
    for other in waiting + fills + [copy]:
        other.wait()

    def add(c, carry):
        acc[smem_names[row, lane + c]] += late[pl.ds(pl.multiple_of(c * sub, sub), sub), :].astype(jnp.float32)
        return carry

    lax.fori_loop(0, cap, add, 0, unroll=4)
    flat = acc.reshape(n_out * sub, LANES)

    def emit(c, carry):
        rows = pl.ds(pl.multiple_of(c * 8, 8), 8)
        for t in range(sub):
            rows_buf[rows, t * LANES:(t + 1) * LANES] = flat[pl.ds(c * (8 * sub) + t, 8, stride=sub), :]
        return carry

    copies = []
    for n, rows in enumerate(blocks):
        lax.fori_loop(n * height // 8, (n + 1) * height // 8, emit, 0)
        copies.append(pltpu.make_async_copy(rows_buf.at[rows], out_ref.at[rows], sems.at[2 + 2 * parts + n]))
        copies[-1].start()
    for copy in copies:
        copy.wait()


def owner_sums(tables, from_b, from_c, sub):
    def whole(x):
        return pl.BlockSpec(x.shape, lambda i: (0,) * len(x.shape))

    table = jax.ShapeDtypeStruct((OSLOT, sub, LANES), jnp.float32)
    names = (NAME_ROWS, LANES)
    early = pl.pallas_call(
        early_kernel,
        out_shape=table,
        grid_spec=pl.GridSpec(
            grid=(1,),
            in_specs=[whole(x) for x in tables],
            out_specs=whole(table),
            scratch_shapes=[pltpu.VMEM(table.shape, jnp.float32)] * len(tables)
            + [
                pltpu.VMEM((len(tables),) + names, jnp.int32),
                pltpu.SMEM((len(tables),) + names, jnp.int32),
                pltpu.SemaphoreType.DMA,
            ],
        ),
        compiler_params=pltpu.CompilerParams(
            dimension_semantics=("arbitrary",), vmem_limit_bytes=20 * 1024 * 1024
        ),
        name="early_sums",
    )(*tables)
    return pl.pallas_call(
        last_kernel,
        out_shape=jax.ShapeDtypeStruct((OSLOT, sub * LANES), jnp.float32),
        grid_spec=pl.GridSpec(
            grid=(1,),
            in_specs=[pl.BlockSpec(memory_space=pl.ANY)] * 3,
            out_specs=pl.BlockSpec(memory_space=pl.ANY),
            scratch_shapes=[
                pltpu.VMEM(table.shape, jnp.float32),
                pltpu.VMEM(from_b.shape, jnp.bfloat16),
                pltpu.VMEM((OSLOT, sub * LANES), jnp.float32),
                pltpu.VMEM(names, jnp.int32),
                pltpu.SMEM(names, jnp.int32),
                pltpu.SemaphoreType.DMA((2 + 3 * 4,)),
            ],
        ),
        compiler_params=pltpu.CompilerParams(
            dimension_semantics=("arbitrary",), vmem_limit_bytes=20 * 1024 * 1024
        ),
        name="owner_sums",
    )(early, from_b, from_c)


def swap(x, axis, d):
    return lax.ppermute(x, axis, [(i, i ^ d) for i in range(lax.axis_size(axis))])


def direct(p_tiles):
    return [swap(p_tiles, "blk", d) for d in range(2, lax.axis_size("blk"), 2)]


def body(a_tiles, a_cols, p_tiles, route_list, out_slot):
    groups = lax.axis_size("grp")
    rf, tile, cols = a_tiles.shape
    cap = out_slot.shape[1] // groups
    sub = tile * tile // LANES
    takes = [(1, 0), (3, 1), (0, 2), (2, 3)]

    def take(x):
        return lax.ppermute(x, "grp", takes)

    rows_sent = with_numbers(a_tiles, route_list, out_slot, a_cols)
    far = direct(p_tiles)
    p_took = take(p_tiles)
    a_took = take(rows_sent)
    far[0], p_took = lax.optimization_barrier((far[0], p_took))
    far_took = direct(p_took)
    mine = [p_tiles, jnp.concatenate(far)]
    other = [swap(x, "blk", 1) for x in mine]

    def tables_own(off, middle):
        return jnp.where(middle, jnp.where(off == 0, 0, jnp.where(off == 1, 3, off - 1)), jnp.where(off < 2, off, 3))

    def tables_took(off, middle):
        return jnp.where((off == 0) | ((off == 1) & middle), off, 2)

    spans = ((0, cap), (cap, cap), (2 * cap, cap))
    own, to_a, to_b = partial_sums(rows_sent, mine + other, tables_own, 3, spans, groups, cap)
    own, p_took, *far_took = lax.optimization_barrier((own, p_took, *far_took))
    to_a, to_b, a_took = lax.optimization_barrier((to_a, to_b, a_took))
    from_a = lax.ppermute(to_a, "grp", [(0, 1), (3, 2), (1, 3), (2, 0)])
    from_b = lax.ppermute(to_b, "grp", [(1, 2), (2, 1)])
    took = [p_took] + far_took
    pieces = took + [swap(x, "blk", 1) for x in took]
    spans = ((0, cap), (cap, cap))
    own_took, to_c = partial_sums(a_took, pieces, tables_took, 2, spans, groups, cap)
    from_c = lax.ppermute(to_c, "grp", [(1, 0), (2, 3)])
    return owner_sums([own, own_took, from_a], from_b, from_c, sub)


def solution(mesh):
    in_specs = (
        P(("blk", "grp"), None, None),
        P(("blk", "grp"), None),
        P(("blk", "grp"), None, None),
        P(("blk", "grp"), None),
        P(("blk", "grp"), None),
    )
    out_specs = P(("blk", "grp"), None)
    return jax.shard_map(body, mesh=mesh, in_specs=in_specs, out_specs=out_specs, check_vma=False)
```

profile of v0, /device:TPU:0, one launch (start us, length us, event | category | flops | bytes accessed | tf_op | source)
XLA Modules:
  0.0 67.3 jit_solution(3549174080319225771)
XLA Ops:
  0.0 0.0 copy-start.1
  0.0 2.9 %collective-permute-start = (bf16[8,64,256]{2,1,0:T(8,128)(2,1)}, bf16[8,64,256]{2,1,0:T(8,128)(2,1)S(1)}, u32[]{:S(2)}, u32[]{:S(2)}) collective-permute-start(bf16[8,64,256]{2,1,0:T(8,128)(2,1)} %refs_0_.1), channel_id=1, source_target_pairs={{0,8},{4,12},{8,0},{12,4},{16,24},{20,28},{24,16},{28,20},{1,9},{5... | collective-permute-start | bytes 786440 | tf_op jit(solution)/shard_map/ppermute | solution.py:410
  2.9 2.6 %collective-permute-start.1 = (bf16[8,64,256]{2,1,0:T(8,128)(2,1)}, bf16[8,64,256]{2,1,0:T(8,128)(2,1)S(1)}, u32[]{:S(2)}, u32[]{:S(2)}) collective-permute-start(bf16[8,64,256]{2,1,0:T(8,128)(2,1)} %refs_0_.1), channel_id=1, source_target_pairs={{1,0},{3,1},{0,2},{2,3},{5,4},{7,5},{4,6},{6,7},{9,8},{11,9},{8,10... | collective-permute-start | bytes 786440 | tf_op jit(solution)/shard_map/ppermute | solution.py:425
  5.5 1.5 %collective-permute-start.2 = (bf16[8,64,256]{2,1,0:T(8,128)(2,1)}, bf16[8,64,256]{2,1,0:T(8,128)(2,1)S(1)}, u32[]{:S(2)}, u32[]{:S(2)}) collective-permute-start(bf16[8,64,256]{2,1,0:T(8,128)(2,1)} %refs_0_.1), channel_id=1, source_target_pairs={{0,16},{4,20},{8,24},{12,28},{16,0},{20,4},{24,8},{28,12},{1,17},{... | collective-permute-start | bytes 786440 | tf_op jit(solution)/shard_map/ppermute | solution.py:410
  7.1 0.5 collective-permute-start.3
  7.5 2.3 %with_numbers.1.rows_in = bf16[528,1024]{1,0:T(8,128)(2,1)} custom-call(bf16[8,64,1024]{2,1,0:T(8,128)(2,1)} %a_ref.1, s32[8,256]{1,0:T(8,128)} %route_ref.1, s32[1,256]{1,0:T(1,128)} %slot_ref.1, s32[8,16]{1,0:T(8,128)} %cols_ref.1), custom_call_target="tpu_custom_call" | custom-call | flops 1 | bytes 1 | tf_op jit(solution)/shard_map/with_numbers/pallas_call | solution.py:41
  9.8 0.0 copy-start
  9.8 1.6 %collective-permute-start.9 = (bf16[528,1024]{1,0:T(8,128)(2,1)}, bf16[528,1024]{1,0:T(8,128)(2,1)S(1)}, u32[]{:S(2)}, u32[]{:S(2)}) collective-permute-start(bf16[528,1024]{1,0:T(8,128)(2,1)} %with_numbers.1.rows_in), channel_id=1, source_target_pairs={{1,0},{3,1},{0,2},{2,3},{5,4},{7,5},{4,6},{6,7},{9,8},{11,9},{8,10... | collective-permute-start | bytes 3244040 | tf_op jit(solution)/shard_map/ppermute | solution.py:425
  11.4 0.0 collective-permute-done
  11.4 0.2 collective-permute-done.1.refs_0_
  11.7 7.2 %collective-permute-done.2 = bf16[8,64,256]{2,1,0:T(8,128)(2,1)S(1)} collective-permute-done((bf16[8,64,256]{2,1,0:T(8,128)(2,1)}, bf16[8,64,256]{2,1,0:T(8,128)(2,1)S(1)}, u32[]{:S(2)}, u32[]{:S(2)}) %collective-permute-start.2) | collective-permute-done | bytes 262176 | tf_op jit(solution)/shard_map/ppermute | solution.py:410
  18.9 0.0 collective-permute-done.3
  18.9 0.1 collective-permute-start.5
  19.0 0.0 copy-done.1
  19.0 0.5 collective-permute-start.4
  19.5 0.5 collective-permute-start.6
  20.0 1.5 %collective-permute-start.7 = (bf16[8,64,256]{2,1,0:T(8,128)(2,1)S(1)}, bf16[8,64,256]{2,1,0:T(8,128)(2,1)S(1)}, u32[]{:S(2)}, u32[]{:S(2)}) collective-permute-start(bf16[8,64,256]{2,1,0:T(8,128)(2,1)S(1)} %collective-permute-done.1.refs_0_), channel_id=1, source_target_pairs={{0,16},{4,20},{8,24},{12,28},{16,0},{20,4},{24,8},{28,12},{1,17},{... | collective-permute-start | bytes 786440 | tf_op jit(solution)/shard_map/ppermute | solution.py:410
  21.5 0.1 collective-permute-done.4.refs_2_
  21.6 1.5 %collective-permute-start.8 = (bf16[8,64,256]{2,1,0:T(8,128)(2,1)S(1)}, bf16[8,64,256]{2,1,0:T(8,128)(2,1)S(1)}, u32[]{:S(2)}, u32[]{:S(2)}) collective-permute-start(bf16[8,64,256]{2,1,0:T(8,128)(2,1)S(1)} %collective-permute-done.1.refs_0_), channel_id=1, source_target_pairs={{0,24},{4,28},{8,16},{12,20},{16,8},{20,12},{24,0},{28,4},{1,25},{... | collective-permute-start | bytes 786440 | tf_op jit(solution)/shard_map/ppermute | solution.py:410
  23.1 0.0 collective-permute-done.5.refs_3_
  23.1 0.0 copy-done
  23.1 9.9 %partial_sums.2 = (bf16[2064,128]{1,0:T(8,128)(2,1)S(1)}, bf16[2064,128]{1,0:T(8,128)(2,1)S(1)}, bf16[2064,128]{1,0:T(8,128)(2,1)S(1)}) custom-call(bf16[528,1024]{1,0:T(8,128)(2,1)S(1)} %copy-done, bf16[8,64,256]{2,1,0:T(8,128)(2,1)S(1)} %copy-done.1, bf16[24,64,256]{2,1,0:T(8,128)(2,1)S(1)} %constant_dynamic-update-slice_fusion.refs_1_, ...), custom_call_target="tpu_custom_call" | custom-call | flops 1 | bytes 1 | tf_op jit(solution)/shard_map/partial_sums/pallas_call | solution.py:225
  33.1 0.0 collective-permute-done.6.refs_1_
  33.1 0.0 collective-permute-done.7.refs_2_
  33.1 1.3 %collective-permute-done.8.refs_3_ = bf16[8,64,256]{2,1,0:T(8,128)(2,1)S(1)} collective-permute-done((bf16[8,64,256]{2,1,0:T(8,128)(2,1)S(1)}, bf16[8,64,256]{2,1,0:T(8,128)(2,1)S(1)}, u32[]{:S(2)}, u32[]{:S(2)}) %collective-permute-start.8) | collective-permute-done | bytes 262176 | tf_op jit(solution)/shard_map/ppermute | solution.py:410
  34.4 0.0 collective-permute-start.10
  34.4 0.5 collective-permute-start.11
  34.9 0.0 collective-permute-start.12
  34.9 0.5 collective-permute-start.13
  35.4 0.0 collective-permute-done.9.rows_in
  35.4 1.2 %collective-permute-start.14 = (bf16[2064,128]{1,0:T(8,128)(2,1)S(1)}, bf16[2064,128]{1,0:T(8,128)(2,1)S(1)}, u32[]{:S(2)}, u32[]{:S(2)}) collective-permute-start(bf16[2064,128]{1,0:T(8,128)(2,1)S(1)} %get-tuple-element.32), channel_id=1, source_target_pairs={{0,1},{3,2},{1,3},{2,0},{4,5},{7,6},{5,7},{6,4},{8,9},{11,10},{9,1... | collective-permute-start | bytes 1585160 | tf_op jit(solution)/shard_map/ppermute | solution.py:446
  36.6 0.0 collective-permute-done.10.refs_4_
  36.6 0.7 %collective-permute-start.15 = (bf16[2064,128]{1,0:T(8,128)(2,1)S(1)}, bf16[2064,128]{1,0:T(8,128)(2,1)S(1)}, u32[]{:S(2)}, u32[]{:S(2)}) collective-permute-start(bf16[2064,128]{1,0:T(8,128)(2,1)S(1)} %get-tuple-element.33), channel_id=1, source_target_pairs={{1,2},{2,1},{5,6},{6,5},{9,10},{10,9},{13,14},{14,13},{17,18},{18,... | collective-permute-start | bytes 1585160 | tf_op jit(solution)/shard_map/ppermute | solution.py:447
  37.3 0.0 collective-permute-done.11.refs_5_
  37.3 0.0 collective-permute-done.12.refs_6_
  37.3 0.0 collective-permute-done.13.refs_7_
  37.3 9.9 %partial_sums.3 = (bf16[2064,128]{1,0:T(8,128)(2,1)S(1)}, bf16[2064,128]{1,0:T(8,128)(2,1)S(1)}) custom-call(bf16[528,1024]{1,0:T(8,128)(2,1)S(1)} %collective-permute-done.9.rows_in, bf16[8,64,256]{2,1,0:T(8,128)(2,1)S(1)} %collective-permute-done.1.refs_0_, bf16[8,64,256]{2,1,0:T(8,128)(2,1)S(1)} %collective-permute-done.6.refs_1_, ...), custom_call_target="tpu_custom_call" | custom-call | flops 1 | bytes 1 | tf_op jit(solution)/shard_map/partial_sums/pallas_call | solution.py:225
  47.2 1.3 %collective-permute-start.16 = (bf16[2064,128]{1,0:T(8,128)(2,1)S(1)}, bf16[2064,128]{1,0:T(8,128)(2,1)S(1)}, u32[]{:S(2)}, u32[]{:S(2)}) collective-permute-start(bf16[2064,128]{1,0:T(8,128)(2,1)S(1)} %get-tuple-element.34), channel_id=1, source_target_pairs={{1,0},{2,3},{5,4},{6,7},{9,8},{10,11},{13,12},{14,15},{17,16},{18,... | collective-permute-start | bytes 1585160 | tf_op jit(solution)/shard_map/ppermute | solution.py:452
  48.5 2.6 %collective-permute-done.14.refs_2_ = bf16[2064,128]{1,0:T(8,128)(2,1)S(1)} collective-permute-done((bf16[2064,128]{1,0:T(8,128)(2,1)S(1)}, bf16[2064,128]{1,0:T(8,128)(2,1)S(1)}, u32[]{:S(2)}, u32[]{:S(2)}) %collective-permute-start.14) | collective-permute-done | bytes 528416 | tf_op jit(solution)/shard_map/ppermute | solution.py:446
  51.2 1.8 %early_sums.1.table = f32[128,32,128]{2,1,0:T(8,128)S(1)} custom-call(bf16[2064,128]{1,0:T(8,128)(2,1)S(1)} %get-tuple-element.23.refs_0_, bf16[2064,128]{1,0:T(8,128)(2,1)S(1)} %get-tuple-element.31.refs_1_, bf16[2064,128]{1,0:T(8,128)(2,1)S(1)} %collective-permute-done.14.refs_2_), custom_call_target="tpu_custom_call" | custom-call | tf_op jit(solution)/shard_map/early_sums/pallas_call | solution.py:367
  53.0 0.0 collective-permute-done.15.from_b
  53.0 10.3 %collective-permute-done.16.from_c = bf16[2064,128]{1,0:T(8,128)(2,1)S(1)} collective-permute-done((bf16[2064,128]{1,0:T(8,128)(2,1)S(1)}, bf16[2064,128]{1,0:T(8,128)(2,1)S(1)}, u32[]{:S(2)}, u32[]{:S(2)}) %collective-permute-start.16) | collective-permute-done | bytes 528416 | tf_op jit(solution)/shard_map/ppermute | solution.py:452
  63.3 4.1 %owner_sums.1 = f32[128,4096]{1,0:T(8,128)} custom-call(f32[128,32,128]{2,1,0:T(8,128)S(1)} %early_sums.1.table, bf16[2064,128]{1,0:T(8,128)(2,1)S(1)} %collective-permute-done.15.from_b, bf16[2064,128]{1,0:T(8,128)(2,1)S(1)} %collective-permute-done.16.from_c), custom_call_target="tpu_custom_call" | custom-call | tf_op jit(solution)/shard_map/owner_sums/pallas_call | solution.py:386
  (3 shorter events, 0.1 us)
Async XLA Ops:
  0.0 19.0 %copy-start.1 = (bf16[8,64,256]{2,1,0:T(8,128)(2,1)S(1)}, bf16[8,64,256]{2,1,0:T(8,128)(2,1)}, u32[]{:S(2)}) copy-start(bf16[8,64,256]{2,1,0:T(8,128)(2,1)} %refs_0_.1) | copy-start | bytes 786436
  0.0 11.4 %collective-permute-start = (bf16[8,64,256]{2,1,0:T(8,128)(2,1)}, bf16[8,64,256]{2,1,0:T(8,128)(2,1)S(1)}, u32[]{:S(2)}, u32[]{:S(2)}) collective-permute-start(bf16[8,64,256]{2,1,0:T(8,128)(2,1)} %refs_0_.1), channel_id=1, source_target_pairs={{0,8},{4,12},{8,0},{12,4},{16,24},{20,28},{24,16},{28,20},{1,9},{5... | collective-permute-start | bytes 786440 | tf_op jit(solution)/shard_map/ppermute | solution.py:410
  2.9 8.7 %collective-permute-start.1 = (bf16[8,64,256]{2,1,0:T(8,128)(2,1)}, bf16[8,64,256]{2,1,0:T(8,128)(2,1)S(1)}, u32[]{:S(2)}, u32[]{:S(2)}) collective-permute-start(bf16[8,64,256]{2,1,0:T(8,128)(2,1)} %refs_0_.1), channel_id=1, source_target_pairs={{1,0},{3,1},{0,2},{2,3},{5,4},{7,5},{4,6},{6,7},{9,8},{11,9},{8,10... | collective-permute-start | bytes 786440 | tf_op jit(solution)/shard_map/ppermute | solution.py:425
  5.5 13.3 %collective-permute-start.2 = (bf16[8,64,256]{2,1,0:T(8,128)(2,1)}, bf16[8,64,256]{2,1,0:T(8,128)(2,1)S(1)}, u32[]{:S(2)}, u32[]{:S(2)}) collective-permute-start(bf16[8,64,256]{2,1,0:T(8,128)(2,1)} %refs_0_.1), channel_id=1, source_target_pairs={{0,16},{4,20},{8,24},{12,28},{16,0},{20,4},{24,8},{28,12},{1,17},{... | collective-permute-start | bytes 786440 | tf_op jit(solution)/shard_map/ppermute | solution.py:410
  7.1 11.8 %collective-permute-start.3 = (bf16[8,64,256]{2,1,0:T(8,128)(2,1)}, bf16[8,64,256]{2,1,0:T(8,128)(2,1)S(1)}, u32[]{:S(2)}, u32[]{:S(2)}) collective-permute-start(bf16[8,64,256]{2,1,0:T(8,128)(2,1)} %refs_0_.1), channel_id=1, source_target_pairs={{0,24},{4,28},{8,16},{12,20},{16,8},{20,12},{24,0},{28,4},{1,25},{... | collective-permute-start | bytes 786440 | tf_op jit(solution)/shard_map/ppermute | solution.py:410
  9.8 13.3 %copy-start = (bf16[528,1024]{1,0:T(8,128)(2,1)S(1)}, bf16[528,1024]{1,0:T(8,128)(2,1)}, u32[]{:S(2)}) copy-start(bf16[528,1024]{1,0:T(8,128)(2,1)} %with_numbers.1.rows_in) | copy-start | bytes 3244036
  9.8 25.5 %collective-permute-start.9 = (bf16[528,1024]{1,0:T(8,128)(2,1)}, bf16[528,1024]{1,0:T(8,128)(2,1)S(1)}, u32[]{:S(2)}, u32[]{:S(2)}) collective-permute-start(bf16[528,1024]{1,0:T(8,128)(2,1)} %with_numbers.1.rows_in), channel_id=1, source_target_pairs={{1,0},{3,1},{0,2},{2,3},{5,4},{7,5},{4,6},{6,7},{9,8},{11,9},{8,10... | collective-permute-start | bytes 3244040 | tf_op jit(solution)/shard_map/ppermute | solution.py:425
  18.9 4.2 %collective-permute-start.5 = (bf16[24,64,256]{2,1,0:T(8,128)(2,1)S(1)}, bf16[24,64,256]{2,1,0:T(8,128)(2,1)S(1)}, u32[]{:S(2)}, u32[]{:S(2)}) collective-permute-start(bf16[24,64,256]{2,1,0:T(8,128)(2,1)S(1)} %constant_dynamic-update-slice_fusion.refs_1_), channel_id=1, source_target_pairs={{0,4},{4,0},{8,12},{12,8},{16,20},{20,16},{24,28},{28,24},{1,5},{5... | collective-permute-start | bytes 2359304 | tf_op jit(solution)/shard_map/ppermute | solution.py:410
  19.0 2.6 %collective-permute-start.4 = (bf16[8,64,256]{2,1,0:T(8,128)(2,1)S(1)}, bf16[8,64,256]{2,1,0:T(8,128)(2,1)S(1)}, u32[]{:S(2)}, u32[]{:S(2)}) collective-permute-start(bf16[8,64,256]{2,1,0:T(8,128)(2,1)S(1)} %copy-done.1), channel_id=1, source_target_pairs={{0,4},{4,0},{8,12},{12,8},{16,20},{20,16},{24,28},{28,24},{1,5},{5... | collective-permute-start | bytes 786440 | tf_op jit(solution)/shard_map/ppermute | solution.py:410
  19.5 13.6 %collective-permute-start.6 = (bf16[8,64,256]{2,1,0:T(8,128)(2,1)S(1)}, bf16[8,64,256]{2,1,0:T(8,128)(2,1)S(1)}, u32[]{:S(2)}, u32[]{:S(2)}) collective-permute-start(bf16[8,64,256]{2,1,0:T(8,128)(2,1)S(1)} %collective-permute-done.1.refs_0_), channel_id=1, source_target_pairs={{0,8},{4,12},{8,0},{12,4},{16,24},{20,28},{24,16},{28,20},{1,9},{5... | collective-permute-start | bytes 786440 | tf_op jit(solution)/shard_map/ppermute | solution.py:410
  20.0 13.0 %collective-permute-start.7 = (bf16[8,64,256]{2,1,0:T(8,128)(2,1)S(1)}, bf16[8,64,256]{2,1,0:T(8,128)(2,1)S(1)}, u32[]{:S(2)}, u32[]{:S(2)}) collective-permute-start(bf16[8,64,256]{2,1,0:T(8,128)(2,1)S(1)} %collective-permute-done.1.refs_0_), channel_id=1, source_target_pairs={{0,16},{4,20},{8,24},{12,28},{16,0},{20,4},{24,8},{28,12},{1,17},{... | collective-permute-start | bytes 786440 | tf_op jit(solution)/shard_map/ppermute | solution.py:410
  21.6 12.7 %collective-permute-start.8 = (bf16[8,64,256]{2,1,0:T(8,128)(2,1)S(1)}, bf16[8,64,256]{2,1,0:T(8,128)(2,1)S(1)}, u32[]{:S(2)}, u32[]{:S(2)}) collective-permute-start(bf16[8,64,256]{2,1,0:T(8,128)(2,1)S(1)} %collective-permute-done.1.refs_0_), channel_id=1, source_target_pairs={{0,24},{4,28},{8,16},{12,20},{16,8},{20,12},{24,0},{28,4},{1,25},{... | collective-permute-start | bytes 786440 | tf_op jit(solution)/shard_map/ppermute | solution.py:410
  34.4 2.2 %collective-permute-start.10 = (bf16[8,64,256]{2,1,0:T(8,128)(2,1)S(1)}, bf16[8,64,256]{2,1,0:T(8,128)(2,1)S(1)}, u32[]{:S(2)}, u32[]{:S(2)}) collective-permute-start(bf16[8,64,256]{2,1,0:T(8,128)(2,1)S(1)} %collective-permute-done.1.refs_0_), channel_id=1, source_target_pairs={{0,4},{4,0},{8,12},{12,8},{16,20},{20,16},{24,28},{28,24},{1,5},{5... | collective-permute-start | bytes 786440 | tf_op jit(solution)/shard_map/ppermute | solution.py:410
  34.4 2.9 %collective-permute-start.11 = (bf16[8,64,256]{2,1,0:T(8,128)(2,1)S(1)}, bf16[8,64,256]{2,1,0:T(8,128)(2,1)S(1)}, u32[]{:S(2)}, u32[]{:S(2)}) collective-permute-start(bf16[8,64,256]{2,1,0:T(8,128)(2,1)S(1)} %collective-permute-done.6.refs_1_), channel_id=1, source_target_pairs={{0,4},{4,0},{8,12},{12,8},{16,20},{20,16},{24,28},{28,24},{1,5},{5... | collective-permute-start | bytes 786440 | tf_op jit(solution)/shard_map/ppermute | solution.py:410
  34.9 2.4 %collective-permute-start.12 = (bf16[8,64,256]{2,1,0:T(8,128)(2,1)S(1)}, bf16[8,64,256]{2,1,0:T(8,128)(2,1)S(1)}, u32[]{:S(2)}, u32[]{:S(2)}) collective-permute-start(bf16[8,64,256]{2,1,0:T(8,128)(2,1)S(1)} %collective-permute-done.7.refs_2_), channel_id=1, source_target_pairs={{0,4},{4,0},{8,12},{12,8},{16,20},{20,16},{24,28},{28,24},{1,5},{5... | collective-permute-start | bytes 786440 | tf_op jit(solution)/shard_map/ppermute | solution.py:410
  34.9 2.4 %collective-permute-start.13 = (bf16[8,64,256]{2,1,0:T(8,128)(2,1)S(1)}, bf16[8,64,256]{2,1,0:T(8,128)(2,1)S(1)}, u32[]{:S(2)}, u32[]{:S(2)}) collective-permute-start(bf16[8,64,256]{2,1,0:T(8,128)(2,1)S(1)} %collective-permute-done.8.refs_3_), channel_id=1, source_target_pairs={{0,4},{4,0},{8,12},{12,8},{16,20},{20,16},{24,28},{28,24},{1,5},{5... | collective-permute-start | bytes 786440 | tf_op jit(solution)/shard_map/ppermute | solution.py:410
  35.4 15.8 %collective-permute-start.14 = (bf16[2064,128]{1,0:T(8,128)(2,1)S(1)}, bf16[2064,128]{1,0:T(8,128)(2,1)S(1)}, u32[]{:S(2)}, u32[]{:S(2)}) collective-permute-start(bf16[2064,128]{1,0:T(8,128)(2,1)S(1)} %get-tuple-element.32), channel_id=1, source_target_pairs={{0,1},{3,2},{1,3},{2,0},{4,5},{7,6},{5,7},{6,4},{8,9},{11,10},{9,1... | collective-permute-start | bytes 1585160 | tf_op jit(solution)/shard_map/ppermute | solution.py:446
  36.6 16.4 %collective-permute-start.15 = (bf16[2064,128]{1,0:T(8,128)(2,1)S(1)}, bf16[2064,128]{1,0:T(8,128)(2,1)S(1)}, u32[]{:S(2)}, u32[]{:S(2)}) collective-permute-start(bf16[2064,128]{1,0:T(8,128)(2,1)S(1)} %get-tuple-element.33), channel_id=1, source_target_pairs={{1,2},{2,1},{5,6},{6,5},{9,10},{10,9},{13,14},{14,13},{17,18},{18,... | collective-permute-start | bytes 1585160 | tf_op jit(solution)/shard_map/ppermute | solution.py:447
  47.2 16.1 %collective-permute-start.16 = (bf16[2064,128]{1,0:T(8,128)(2,1)S(1)}, bf16[2064,128]{1,0:T(8,128)(2,1)S(1)}, u32[]{:S(2)}, u32[]{:S(2)}) collective-permute-start(bf16[2064,128]{1,0:T(8,128)(2,1)S(1)} %get-tuple-element.34), channel_id=1, source_target_pairs={{1,0},{2,3},{5,4},{6,7},{9,8},{10,11},{13,12},{14,15},{17,16},{18,... | collective-permute-start | bytes 1585160 | tf_op jit(solution)/shard_map/ppermute | solution.py:452
where the time goes:
time: 67.5 us; the launch traced here: 67.3 us
  Pallas kernels  28 us (41%)
  waiting for transfers between devices  21.7 us (32%)
  starting transfers between devices  17.4 us (26%)
    pallas_call x2, Pallas kernels, partial_sums(): pl.pallas_call(functools.partial(partial_kernel, len(pieces), spans, cap,...  19.8 us
    ppermute x1, waiting for transfers between devices, body(): from_c = lax.ppermute(to_c, 'grp', [(1, 0), (2, 3)])  10.3 us
    ppermute x12, starting transfers between devices, swap(): lax.ppermute(x, axis, [(i, i ^ d) for i in range(lax.axis_size(axis))])  10.1 us
    ppermute x12, waiting for transfers between devices, swap(): lax.ppermute(x, axis, [(i, i ^ d) for i in range(lax.axis_size(axis))])  8.58 us
    ppermute x2, starting transfers between devices, take(): return lax.ppermute(x, 'grp', takes)  4.17 us
    pallas_call x1, Pallas kernels, owner_sums(): pl.pallas_call(last_kernel, out_shape=jax.ShapeDtypeStruct((OSLOT, sub *...  4.06 us
    ppermute x1, waiting for transfers between devices, body(): from_a = lax.ppermute(to_a, 'grp', [(0, 1), (3, 2), (1, 3), (2, 0)])  2.64 us
    pallas_call x1, Pallas kernels, with_numbers(): pl.pallas_call(numbers_kernel, out_shape=jax.ShapeDtypeStruct((rf * tile...  2.3 us
  transfers between devices with their start and end apart: 17, of which 6 were waited for; matrix products, arithmetic and copies ran while one was open for 0% of the time, Pallas kernels for 36%

commit v1 on v0

--- a/solution.py
+++ b/solution.py
@@ -25,23 +25,43 @@
     return 0, n_places, 2 * n_places, 2 * n_places + LANES
 
 
-def numbers_kernel(a_ref, route_ref, slot_ref, cols_ref, out_ref, wide):
-    rf, tile, width = a_ref.shape
-    out_ref[:rf * tile, :] = a_ref[...].reshape(rf * tile, width)
+def numbers_kernel(a_ref, route_ref, slot_ref, cols_ref, out_ref, held, wide, packed, sems):
+    rf, tile, _ = a_ref.shape
+    into, out = [], []
+    for n in range(rf):
+        rows = pl.ds(n * tile, tile)
+        into.append(pltpu.make_async_copy(a_ref.at[n], held.at[n], sems.at[n]))
+        out.append(pltpu.make_async_copy(held.at[n], out_ref.at[rows], sems.at[rf + n]))
+        into[-1].start()
     wide[...] = jnp.zeros_like(wide)
     cols = cols_ref[...]
     parts = (route_ref[...], slot_ref[...], lax.shift_right_logical(cols, jnp.int32(log2(PART))), cols & (PART - 1))
     for at, part in zip(number_columns(route_ref.shape[1]), parts):
         wide[:part.shape[0], at:at + part.shape[1]] = part.astype(jnp.float32)
-    out_ref[rf * tile:, :] = wide[...].astype(out_ref.dtype)
+    packed[...] = wide[...].astype(packed.dtype)
+    last = pltpu.make_async_copy(packed, out_ref.at[pl.ds(rf * tile, NAME_ROWS)], sems.at[2 * rf])
+    last.start()
+    for arriving, leaving in zip(into, out):
+        arriving.wait()
+        leaving.start()
+    for copy in out + [last]:
+        copy.wait()
 
 
 def with_numbers(a_tiles, route_list, out_slot, a_cols):
     rf, tile, width = a_tiles.shape
+    whole = pl.BlockSpec(memory_space=pltpu.VMEM)
     return pl.pallas_call(
         numbers_kernel,
         out_shape=jax.ShapeDtypeStruct((rf * tile + NAME_ROWS, width), a_tiles.dtype),
-        scratch_shapes=[pltpu.VMEM((NAME_ROWS, width), jnp.float32)],
+        in_specs=[pl.BlockSpec(memory_space=pl.ANY)] + [whole] * 3,
+        out_specs=pl.BlockSpec(memory_space=pl.ANY),
+        scratch_shapes=[
+            pltpu.VMEM(a_tiles.shape, a_tiles.dtype),
+            pltpu.VMEM((NAME_ROWS, width), jnp.float32),
+            pltpu.VMEM((NAME_ROWS, width), a_tiles.dtype),
+            pltpu.SemaphoreType.DMA((2 * rf + 1,)),
+        ],
         compiler_params=pltpu.CompilerParams(vmem_limit_bytes=56 * 1024 * 1024),
         cost_estimate=pl.CostEstimate(flops=1, bytes_accessed=1, transcendentals=0),
         name="with_numbers",
@@ -442,13 +462,14 @@
     spans = ((0, cap), (cap, cap), (2 * cap, cap))
     own, to_a, to_b = partial_sums(rows_sent, mine + other, tables_own, 3, spans, groups, cap)
     own, p_took, *far_took = lax.optimization_barrier((own, p_took, *far_took))
-    to_a, to_b, a_took = lax.optimization_barrier((to_a, to_b, a_took))
+    to_a, a_took = lax.optimization_barrier((to_a, a_took))
     from_a = lax.ppermute(to_a, "grp", [(0, 1), (3, 2), (1, 3), (2, 0)])
-    from_b = lax.ppermute(to_b, "grp", [(1, 2), (2, 1)])
     took = [p_took] + far_took
     pieces = took + [swap(x, "blk", 1) for x in took]
     spans = ((0, cap), (cap, cap))
     own_took, to_c = partial_sums(a_took, pieces, tables_took, 2, spans, groups, cap)
+    to_b, to_c = lax.optimization_barrier((to_b, to_c))
+    from_b = lax.ppermute(to_b, "grp", [(1, 2), (2, 1)])
     from_c = lax.ppermute(to_c, "grp", [(1, 0), (2, 3)])
     return owner_sums([own, own_took, from_a], from_b, from_c, sub)
 

time: 67.5 us -> 68.2 us (1.010)
    ppermute x1, waiting for transfers between devices: 10.3 us -> 11.9 us  [body(): from_c = lax.ppermute(to_c, 'grp', [(1, 0), (2, 3)])]
    ppermute x1, waiting for transfers between devices: 2.64 us -> 1.33 us  [body(): from_a = lax.ppermute(to_a, 'grp', [(0, 1), (3, 2), (1, 3), (2, 0)])]
where the time goes in v1:
time: 68.2 us; the launch traced here: 68 us
  Pallas kernels  28.5 us (42%)
  waiting for transfers between devices  21.8 us (32%)
  starting transfers between devices  17.5 us (26%)
    pallas_call x2, Pallas kernels, partial_sums(): pl.pallas_call(functools.partial(partial_kernel, len(pieces), spans, cap,...  19.8 us
    ppermute x1, waiting for transfers between devices, body(): from_c = lax.ppermute(to_c, 'grp', [(1, 0), (2, 3)])  11.9 us
    ppermute x12, starting transfers between devices, swap(): lax.ppermute(x, axis, [(i, i ^ d) for i in range(lax.axis_size(axis))])  10.1 us
    ppermute x12, waiting for transfers between devices, swap(): lax.ppermute(x, axis, [(i, i ^ d) for i in range(lax.axis_size(axis))])  8.62 us
    ppermute x2, starting transfers between devices, take(): return lax.ppermute(x, 'grp', takes)  4.22 us
    pallas_call x1, Pallas kernels, owner_sums(): pl.pallas_call(last_kernel, out_shape=jax.ShapeDtypeStruct((OSLOT, sub *...  4.06 us
    pallas_call x1, Pallas kernels, with_numbers(): pl.pallas_call(numbers_kernel, out_shape=jax.ShapeDtypeStruct((rf * tile...  2.83 us
    pallas_call x1, Pallas kernels, owner_sums(): pl.pallas_call(early_kernel, out_shape=table, grid_spec=pl.GridSpec(grid=...  1.82 us
  transfers between devices with their start and end apart: 17, of which 6 were waited for; matrix products, arithmetic and copies ran while one was open for 0% of the time, Pallas kernels for 36%

profile of v1, /device:TPU:0, one launch (start us, length us, event | category | flops | bytes accessed | tf_op | source)
XLA Modules:
  0.0 68.0 jit_solution(16058281293901064434)
XLA Ops:
  0.0 0.0 copy-start.1
  0.0 2.9 %collective-permute-start = (bf16[8,64,256]{2,1,0:T(8,128)(2,1)}, bf16[8,64,256]{2,1,0:T(8,128)(2,1)S(1)}, u32[]{:S(2)}, u32[]{:S(2)}) collective-permute-start(bf16[8,64,256]{2,1,0:T(8,128)(2,1)} %refs_0_.1), channel_id=1, source_target_pairs={{0,8},{4,12},{8,0},{12,4},{16,24},{20,28},{24,16},{28,20},{1,9},{5... | collective-permute-start | bytes 786440 | tf_op jit(solution)/shard_map/ppermute | solution.py:430
  2.9 2.6 %collective-permute-start.1 = (bf16[8,64,256]{2,1,0:T(8,128)(2,1)}, bf16[8,64,256]{2,1,0:T(8,128)(2,1)S(1)}, u32[]{:S(2)}, u32[]{:S(2)}) collective-permute-start(bf16[8,64,256]{2,1,0:T(8,128)(2,1)} %refs_0_.1), channel_id=1, source_target_pairs={{1,0},{3,1},{0,2},{2,3},{5,4},{7,5},{4,6},{6,7},{9,8},{11,9},{8,10... | collective-permute-start | bytes 786440 | tf_op jit(solution)/shard_map/ppermute | solution.py:445
  5.5 1.5 %collective-permute-start.2 = (bf16[8,64,256]{2,1,0:T(8,128)(2,1)}, bf16[8,64,256]{2,1,0:T(8,128)(2,1)S(1)}, u32[]{:S(2)}, u32[]{:S(2)}) collective-permute-start(bf16[8,64,256]{2,1,0:T(8,128)(2,1)} %refs_0_.1), channel_id=1, source_target_pairs={{0,16},{4,20},{8,24},{12,28},{16,0},{20,4},{24,8},{28,12},{1,17},{... | collective-permute-start | bytes 786440 | tf_op jit(solution)/shard_map/ppermute | solution.py:430
  7.1 0.5 collective-permute-start.3
  7.5 2.8 %with_numbers.1.rows_in = bf16[528,1024]{1,0:T(8,128)(2,1)} custom-call(bf16[8,64,1024]{2,1,0:T(8,128)(2,1)} %a_ref.1, s32[8,256]{1,0:T(8,128)} %route_ref.1, s32[1,256]{1,0:T(1,128)} %slot_ref.1, s32[8,16]{1,0:T(8,128)} %cols_ref.1), custom_call_target="tpu_custom_call" | custom-call | flops 1 | bytes 1 | tf_op jit(solution)/shard_map/with_numbers/pallas_call | solution.py:54
  10.4 0.0 copy-start
  10.4 1.6 %collective-permute-start.9 = (bf16[528,1024]{1,0:T(8,128)(2,1)}, bf16[528,1024]{1,0:T(8,128)(2,1)S(1)}, u32[]{:S(2)}, u32[]{:S(2)}) collective-permute-start(bf16[528,1024]{1,0:T(8,128)(2,1)} %with_numbers.1.rows_in), channel_id=1, source_target_pairs={{1,0},{3,1},{0,2},{2,3},{5,4},{7,5},{4,6},{6,7},{9,8},{11,9},{8,10... | collective-permute-start | bytes 3244040 | tf_op jit(solution)/shard_map/ppermute | solution.py:445
  12.0 0.0 collective-permute-done
  12.0 0.0 collective-permute-done.1.refs_0_
  12.0 6.8 %collective-permute-done.2 = bf16[8,64,256]{2,1,0:T(8,128)(2,1)S(1)} collective-permute-done((bf16[8,64,256]{2,1,0:T(8,128)(2,1)}, bf16[8,64,256]{2,1,0:T(8,128)(2,1)S(1)}, u32[]{:S(2)}, u32[]{:S(2)}) %collective-permute-start.2) | collective-permute-done | bytes 262176 | tf_op jit(solution)/shard_map/ppermute | solution.py:430
  18.9 0.0 collective-permute-done.3
  18.9 0.1 collective-permute-start.5
  19.0 0.0 copy-done.1
  19.0 0.5 collective-permute-start.4
  19.5 0.5 collective-permute-start.6
  20.0 1.5 %collective-permute-start.7 = (bf16[8,64,256]{2,1,0:T(8,128)(2,1)S(1)}, bf16[8,64,256]{2,1,0:T(8,128)(2,1)S(1)}, u32[]{:S(2)}, u32[]{:S(2)}) collective-permute-start(bf16[8,64,256]{2,1,0:T(8,128)(2,1)S(1)} %collective-permute-done.1.refs_0_), channel_id=1, source_target_pairs={{0,16},{4,20},{8,24},{12,28},{16,0},{20,4},{24,8},{28,12},{1,17},{... | collective-permute-start | bytes 786440 | tf_op jit(solution)/shard_map/ppermute | solution.py:430
  21.5 0.1 collective-permute-done.4.refs_2_
  21.6 1.5 %collective-permute-start.8 = (bf16[8,64,256]{2,1,0:T(8,128)(2,1)S(1)}, bf16[8,64,256]{2,1,0:T(8,128)(2,1)S(1)}, u32[]{:S(2)}, u32[]{:S(2)}) collective-permute-start(bf16[8,64,256]{2,1,0:T(8,128)(2,1)S(1)} %collective-permute-done.1.refs_0_), channel_id=1, source_target_pairs={{0,24},{4,28},{8,16},{12,20},{16,8},{20,12},{24,0},{28,4},{1,25},{... | collective-permute-start | bytes 786440 | tf_op jit(solution)/shard_map/ppermute | solution.py:430
  23.1 0.0 collective-permute-done.5.refs_3_
  23.1 0.0 copy-done
  23.1 9.9 %partial_sums.2 = (bf16[2064,128]{1,0:T(8,128)(2,1)S(1)}, bf16[2064,128]{1,0:T(8,128)(2,1)S(1)}, bf16[2064,128]{1,0:T(8,128)(2,1)S(1)}) custom-call(bf16[528,1024]{1,0:T(8,128)(2,1)S(1)} %copy-done, bf16[8,64,256]{2,1,0:T(8,128)(2,1)S(1)} %copy-done.1, bf16[24,64,256]{2,1,0:T(8,128)(2,1)S(1)} %constant_dynamic-update-slice_fusion.refs_1_, ...), custom_call_target="tpu_custom_call" | custom-call | flops 1 | bytes 1 | tf_op jit(solution)/shard_map/partial_sums/pallas_call | solution.py:245
  33.1 0.0 collective-permute-done.6.refs_1_
  33.1 0.0 collective-permute-done.7.refs_2_
  33.1 1.3 %collective-permute-done.8.refs_3_ = bf16[8,64,256]{2,1,0:T(8,128)(2,1)S(1)} collective-permute-done((bf16[8,64,256]{2,1,0:T(8,128)(2,1)S(1)}, bf16[8,64,256]{2,1,0:T(8,128)(2,1)S(1)}, u32[]{:S(2)}, u32[]{:S(2)}) %collective-permute-start.8) | collective-permute-done | bytes 262176 | tf_op jit(solution)/shard_map/ppermute | solution.py:430
  34.4 0.0 collective-permute-start.10
  34.4 0.5 collective-permute-start.11
  34.9 0.0 collective-permute-start.12
  34.9 0.5 collective-permute-start.13
  35.4 0.0 collective-permute-done.9.rows_in
  35.4 1.2 %collective-permute-start.14 = (bf16[2064,128]{1,0:T(8,128)(2,1)S(1)}, bf16[2064,128]{1,0:T(8,128)(2,1)S(1)}, u32[]{:S(2)}, u32[]{:S(2)}) collective-permute-start(bf16[2064,128]{1,0:T(8,128)(2,1)S(1)} %get-tuple-element.32), channel_id=1, source_target_pairs={{0,1},{3,2},{1,3},{2,0},{4,5},{7,6},{5,7},{6,4},{8,9},{11,10},{9,1... | collective-permute-start | bytes 1585160 | tf_op jit(solution)/shard_map/ppermute | solution.py:466
  36.6 0.0 collective-permute-done.10.refs_4_
  36.6 0.0 collective-permute-done.11.refs_5_
  36.6 0.1 collective-permute-done.12.refs_6_
  36.6 0.4 collective-permute-done.13.refs_7_
  37.0 9.8 %partial_sums.3 = (bf16[2064,128]{1,0:T(8,128)(2,1)S(1)}, bf16[2064,128]{1,0:T(8,128)(2,1)S(1)}) custom-call(bf16[528,1024]{1,0:T(8,128)(2,1)S(1)} %collective-permute-done.9.rows_in, bf16[8,64,256]{2,1,0:T(8,128)(2,1)S(1)} %collective-permute-done.1.refs_0_, bf16[8,64,256]{2,1,0:T(8,128)(2,1)S(1)} %collective-permute-done.6.refs_1_, ...), custom_call_target="tpu_custom_call" | custom-call | flops 1 | bytes 1 | tf_op jit(solution)/shard_map/partial_sums/pallas_call | solution.py:245
  46.9 0.7 %collective-permute-start.15 = (bf16[2064,128]{1,0:T(8,128)(2,1)S(1)}, bf16[2064,128]{1,0:T(8,128)(2,1)S(1)}, u32[]{:S(2)}, u32[]{:S(2)}) collective-permute-start(bf16[2064,128]{1,0:T(8,128)(2,1)S(1)} %get-tuple-element.35), channel_id=1, source_target_pairs={{1,2},{2,1},{5,6},{6,5},{9,10},{10,9},{13,14},{14,13},{17,18},{18,... | collective-permute-start | bytes 1585160 | tf_op jit(solution)/shard_map/ppermute | solution.py:472
  47.6 1.3 %collective-permute-start.16 = (bf16[2064,128]{1,0:T(8,128)(2,1)S(1)}, bf16[2064,128]{1,0:T(8,128)(2,1)S(1)}, u32[]{:S(2)}, u32[]{:S(2)}) collective-permute-start(bf16[2064,128]{1,0:T(8,128)(2,1)S(1)} %get-tuple-element.36), channel_id=1, source_target_pairs={{1,0},{2,3},{5,4},{6,7},{9,8},{10,11},{13,12},{14,15},{17,16},{18,... | collective-permute-start | bytes 1585160 | tf_op jit(solution)/shard_map/ppermute | solution.py:473
  48.9 1.3 %collective-permute-done.14.refs_2_ = bf16[2064,128]{1,0:T(8,128)(2,1)S(1)} collective-permute-done((bf16[2064,128]{1,0:T(8,128)(2,1)S(1)}, bf16[2064,128]{1,0:T(8,128)(2,1)S(1)}, u32[]{:S(2)}, u32[]{:S(2)}) %collective-permute-start.14) | collective-permute-done | bytes 528416 | tf_op jit(solution)/shard_map/ppermute | solution.py:466
  50.2 1.8 %early_sums.1.table = f32[128,32,128]{2,1,0:T(8,128)S(1)} custom-call(bf16[2064,128]{1,0:T(8,128)(2,1)S(1)} %get-tuple-element.24.refs_0_, bf16[2064,128]{1,0:T(8,128)(2,1)S(1)} %get-tuple-element.31.refs_1_, bf16[2064,128]{1,0:T(8,128)(2,1)S(1)} %collective-permute-done.14.refs_2_), custom_call_target="tpu_custom_call" | custom-call | tf_op jit(solution)/shard_map/early_sums/pallas_call | solution.py:387
  52.0 0.0 collective-permute-done.15.from_b
  52.0 11.9 %collective-permute-done.16.from_c = bf16[2064,128]{1,0:T(8,128)(2,1)S(1)} collective-permute-done((bf16[2064,128]{1,0:T(8,128)(2,1)S(1)}, bf16[2064,128]{1,0:T(8,128)(2,1)S(1)}, u32[]{:S(2)}, u32[]{:S(2)}) %collective-permute-start.16) | collective-permute-done | bytes 528416 | tf_op jit(solution)/shard_map/ppermute | solution.py:473
  63.9 4.1 %owner_sums.1 = f32[128,4096]{1,0:T(8,128)} custom-call(f32[128,32,128]{2,1,0:T(8,128)S(1)} %early_sums.1.table, bf16[2064,128]{1,0:T(8,128)(2,1)S(1)} %collective-permute-done.15.from_b, bf16[2064,128]{1,0:T(8,128)(2,1)S(1)} %collective-permute-done.16.from_c), custom_call_target="tpu_custom_call" | custom-call | tf_op jit(solution)/shard_map/owner_sums/pallas_call | solution.py:406
  (3 shorter events, 0.1 us)
Async XLA Ops:
  0.0 19.0 %copy-start.1 = (bf16[8,64,256]{2,1,0:T(8,128)(2,1)S(1)}, bf16[8,64,256]{2,1,0:T(8,128)(2,1)}, u32[]{:S(2)}) copy-start(bf16[8,64,256]{2,1,0:T(8,128)(2,1)} %refs_0_.1) | copy-start | bytes 786436
  0.0 12.0 %collective-permute-start = (bf16[8,64,256]{2,1,0:T(8,128)(2,1)}, bf16[8,64,256]{2,1,0:T(8,128)(2,1)S(1)}, u32[]{:S(2)}, u32[]{:S(2)}) collective-permute-start(bf16[8,64,256]{2,1,0:T(8,128)(2,1)} %refs_0_.1), channel_id=1, source_target_pairs={{0,8},{4,12},{8,0},{12,4},{16,24},{20,28},{24,16},{28,20},{1,9},{5... | collective-permute-start | bytes 786440 | tf_op jit(solution)/shard_map/ppermute | solution.py:430
  2.9 9.1 %collective-permute-start.1 = (bf16[8,64,256]{2,1,0:T(8,128)(2,1)}, bf16[8,64,256]{2,1,0:T(8,128)(2,1)S(1)}, u32[]{:S(2)}, u32[]{:S(2)}) collective-permute-start(bf16[8,64,256]{2,1,0:T(8,128)(2,1)} %refs_0_.1), channel_id=1, source_target_pairs={{1,0},{3,1},{0,2},{2,3},{5,4},{7,5},{4,6},{6,7},{9,8},{11,9},{8,10... | collective-permute-start | bytes 786440 | tf_op jit(solution)/shard_map/ppermute | solution.py:445
  5.5 13.3 %collective-permute-start.2 = (bf16[8,64,256]{2,1,0:T(8,128)(2,1)}, bf16[8,64,256]{2,1,0:T(8,128)(2,1)S(1)}, u32[]{:S(2)}, u32[]{:S(2)}) collective-permute-start(bf16[8,64,256]{2,1,0:T(8,128)(2,1)} %refs_0_.1), channel_id=1, source_target_pairs={{0,16},{4,20},{8,24},{12,28},{16,0},{20,4},{24,8},{28,12},{1,17},{... | collective-permute-start | bytes 786440 | tf_op jit(solution)/shard_map/ppermute | solution.py:430
  7.1 11.8 %collective-permute-start.3 = (bf16[8,64,256]{2,1,0:T(8,128)(2,1)}, bf16[8,64,256]{2,1,0:T(8,128)(2,1)S(1)}, u32[]{:S(2)}, u32[]{:S(2)}) collective-permute-start(bf16[8,64,256]{2,1,0:T(8,128)(2,1)} %refs_0_.1), channel_id=1, source_target_pairs={{0,24},{4,28},{8,16},{12,20},{16,8},{20,12},{24,0},{28,4},{1,25},{... | collective-permute-start | bytes 786440 | tf_op jit(solution)/shard_map/ppermute | solution.py:430
  10.4 12.8 %copy-start = (bf16[528,1024]{1,0:T(8,128)(2,1)S(1)}, bf16[528,1024]{1,0:T(8,128)(2,1)}, u32[]{:S(2)}) copy-start(bf16[528,1024]{1,0:T(8,128)(2,1)} %with_numbers.1.rows_in) | copy-start | bytes 3244036
  10.4 25.0 %collective-permute-start.9 = (bf16[528,1024]{1,0:T(8,128)(2,1)}, bf16[528,1024]{1,0:T(8,128)(2,1)S(1)}, u32[]{:S(2)}, u32[]{:S(2)}) collective-permute-start(bf16[528,1024]{1,0:T(8,128)(2,1)} %with_numbers.1.rows_in), channel_id=1, source_target_pairs={{1,0},{3,1},{0,2},{2,3},{5,4},{7,5},{4,6},{6,7},{9,8},{11,9},{8,10... | collective-permute-start | bytes 3244040 | tf_op jit(solution)/shard_map/ppermute | solution.py:445
  18.9 4.2 %collective-permute-start.5 = (bf16[24,64,256]{2,1,0:T(8,128)(2,1)S(1)}, bf16[24,64,256]{2,1,0:T(8,128)(2,1)S(1)}, u32[]{:S(2)}, u32[]{:S(2)}) collective-permute-start(bf16[24,64,256]{2,1,0:T(8,128)(2,1)S(1)} %constant_dynamic-update-slice_fusion.refs_1_), channel_id=1, source_target_pairs={{0,4},{4,0},{8,12},{12,8},{16,20},{20,16},{24,28},{28,24},{1,5},{5... | collective-permute-start | bytes 2359304 | tf_op jit(solution)/shard_map/ppermute | solution.py:430
  19.0 2.6 %collective-permute-start.4 = (bf16[8,64,256]{2,1,0:T(8,128)(2,1)S(1)}, bf16[8,64,256]{2,1,0:T(8,128)(2,1)S(1)}, u32[]{:S(2)}, u32[]{:S(2)}) collective-permute-start(bf16[8,64,256]{2,1,0:T(8,128)(2,1)S(1)} %copy-done.1), channel_id=1, source_target_pairs={{0,4},{4,0},{8,12},{12,8},{16,20},{20,16},{24,28},{28,24},{1,5},{5... | collective-permute-start | bytes 786440 | tf_op jit(solution)/shard_map/ppermute | solution.py:430
  19.5 13.6 %collective-permute-start.6 = (bf16[8,64,256]{2,1,0:T(8,128)(2,1)S(1)}, bf16[8,64,256]{2,1,0:T(8,128)(2,1)S(1)}, u32[]{:S(2)}, u32[]{:S(2)}) collective-permute-start(bf16[8,64,256]{2,1,0:T(8,128)(2,1)S(1)} %collective-permute-done.1.refs_0_), channel_id=1, source_target_pairs={{0,8},{4,12},{8,0},{12,4},{16,24},{20,28},{24,16},{28,20},{1,9},{5... | collective-permute-start | bytes 786440 | tf_op jit(solution)/shard_map/ppermute | solution.py:430
  20.0 13.1 %collective-permute-start.7 = (bf16[8,64,256]{2,1,0:T(8,128)(2,1)S(1)}, bf16[8,64,256]{2,1,0:T(8,128)(2,1)S(1)}, u32[]{:S(2)}, u32[]{:S(2)}) collective-permute-start(bf16[8,64,256]{2,1,0:T(8,128)(2,1)S(1)} %collective-permute-done.1.refs_0_), channel_id=1, source_target_pairs={{0,16},{4,20},{8,24},{12,28},{16,0},{20,4},{24,8},{28,12},{1,17},{... | collective-permute-start | bytes 786440 | tf_op jit(solution)/shard_map/ppermute | solution.py:430
  21.6 12.7 %collective-permute-start.8 = (bf16[8,64,256]{2,1,0:T(8,128)(2,1)S(1)}, bf16[8,64,256]{2,1,0:T(8,128)(2,1)S(1)}, u32[]{:S(2)}, u32[]{:S(2)}) collective-permute-start(bf16[8,64,256]{2,1,0:T(8,128)(2,1)S(1)} %collective-permute-done.1.refs_0_), channel_id=1, source_target_pairs={{0,24},{4,28},{8,16},{12,20},{16,8},{20,12},{24,0},{28,4},{1,25},{... | collective-permute-start | bytes 786440 | tf_op jit(solution)/shard_map/ppermute | solution.py:430
  34.4 2.2 %collective-permute-start.10 = (bf16[8,64,256]{2,1,0:T(8,128)(2,1)S(1)}, bf16[8,64,256]{2,1,0:T(8,128)(2,1)S(1)}, u32[]{:S(2)}, u32[]{:S(2)}) collective-permute-start(bf16[8,64,256]{2,1,0:T(8,128)(2,1)S(1)} %collective-permute-done.1.refs_0_), channel_id=1, source_target_pairs={{0,4},{4,0},{8,12},{12,8},{16,20},{20,16},{24,28},{28,24},{1,5},{5... | collective-permute-start | bytes 786440 | tf_op jit(solution)/shard_map/ppermute | solution.py:430
  34.4 2.2 %collective-permute-start.11 = (bf16[8,64,256]{2,1,0:T(8,128)(2,1)S(1)}, bf16[8,64,256]{2,1,0:T(8,128)(2,1)S(1)}, u32[]{:S(2)}, u32[]{:S(2)}) collective-permute-start(bf16[8,64,256]{2,1,0:T(8,128)(2,1)S(1)} %collective-permute-done.6.refs_1_), channel_id=1, source_target_pairs={{0,4},{4,0},{8,12},{12,8},{16,20},{20,16},{24,28},{28,24},{1,5},{5... | collective-permute-start | bytes 786440 | tf_op jit(solution)/shard_map/ppermute | solution.py:430
  34.9 1.8 %collective-permute-start.12 = (bf16[8,64,256]{2,1,0:T(8,128)(2,1)S(1)}, bf16[8,64,256]{2,1,0:T(8,128)(2,1)S(1)}, u32[]{:S(2)}, u32[]{:S(2)}) collective-permute-start(bf16[8,64,256]{2,1,0:T(8,128)(2,1)S(1)} %collective-permute-done.7.refs_2_), channel_id=1, source_target_pairs={{0,4},{4,0},{8,12},{12,8},{16,20},{20,16},{24,28},{28,24},{1,5},{5... | collective-permute-start | bytes 786440 | tf_op jit(solution)/shard_map/ppermute | solution.py:430
  34.9 2.1 %collective-permute-start.13 = (bf16[8,64,256]{2,1,0:T(8,128)(2,1)S(1)}, bf16[8,64,256]{2,1,0:T(8,128)(2,1)S(1)}, u32[]{:S(2)}, u32[]{:S(2)}) collective-permute-start(bf16[8,64,256]{2,1,0:T(8,128)(2,1)S(1)} %collective-permute-done.8.refs_3_), channel_id=1, source_target_pairs={{0,4},{4,0},{8,12},{12,8},{16,20},{20,16},{24,28},{28,24},{1,5},{5... | collective-permute-start | bytes 786440 | tf_op jit(solution)/shard_map/ppermute | solution.py:430
  35.4 14.8 %collective-permute-start.14 = (bf16[2064,128]{1,0:T(8,128)(2,1)S(1)}, bf16[2064,128]{1,0:T(8,128)(2,1)S(1)}, u32[]{:S(2)}, u32[]{:S(2)}) collective-permute-start(bf16[2064,128]{1,0:T(8,128)(2,1)S(1)} %get-tuple-element.32), channel_id=1, source_target_pairs={{0,1},{3,2},{1,3},{2,0},{4,5},{7,6},{5,7},{6,4},{8,9},{11,10},{9,1... | collective-permute-start | bytes 1585160 | tf_op jit(solution)/shard_map/ppermute | solution.py:466
  46.9 5.2 %collective-permute-start.15 = (bf16[2064,128]{1,0:T(8,128)(2,1)S(1)}, bf16[2064,128]{1,0:T(8,128)(2,1)S(1)}, u32[]{:S(2)}, u32[]{:S(2)}) collective-permute-start(bf16[2064,128]{1,0:T(8,128)(2,1)S(1)} %get-tuple-element.35), channel_id=1, source_target_pairs={{1,2},{2,1},{5,6},{6,5},{9,10},{10,9},{13,14},{14,13},{17,18},{18,... | collective-permute-start | bytes 1585160 | tf_op jit(solution)/shard_map/ppermute | solution.py:472
  47.6 16.3 %collective-permute-start.16 = (bf16[2064,128]{1,0:T(8,128)(2,1)S(1)}, bf16[2064,128]{1,0:T(8,128)(2,1)S(1)}, u32[]{:S(2)}, u32[]{:S(2)}) collective-permute-start(bf16[2064,128]{1,0:T(8,128)(2,1)S(1)} %get-tuple-element.36), channel_id=1, source_target_pairs={{1,0},{2,3},{5,4},{6,7},{9,8},{10,11},{13,12},{14,15},{17,16},{18,... | collective-permute-start | bytes 1585160 | tf_op jit(solution)/shard_map/ppermute | solution.py:473

commit v2 on v0

--- a/solution.py
+++ b/solution.py
@@ -294,7 +294,7 @@
     lax.fori_loop(0, n_out // chunk, merge, 0)
 
 
-def last_kernel(table, from_b, from_c, out_ref, acc, late, rows_buf, vmem_names, smem_names, sems):
+def last_kernel(table, from_c, from_b, out_ref, acc, late, rows_buf, vmem_names, smem_names, sems):
     n_out, sub = acc.shape[:2]
     cap = (late.shape[0] - NAME_ROWS) // sub
     me = lax.axis_index("grp")
@@ -358,7 +358,7 @@
         copy.wait()
 
 
-def owner_sums(tables, from_b, from_c, sub):
+def owner_sums(tables, from_c, from_b, sub):
     def whole(x):
         return pl.BlockSpec(x.shape, lambda i: (0,) * len(x.shape))
 
@@ -403,7 +403,7 @@
             dimension_semantics=("arbitrary",), vmem_limit_bytes=20 * 1024 * 1024
         ),
         name="owner_sums",
-    )(early, from_b, from_c)
+    )(early, from_c, from_b)
 
 
 def swap(x, axis, d):
@@ -442,15 +442,16 @@
     spans = ((0, cap), (cap, cap), (2 * cap, cap))
     own, to_a, to_b = partial_sums(rows_sent, mine + other, tables_own, 3, spans, groups, cap)
     own, p_took, *far_took = lax.optimization_barrier((own, p_took, *far_took))
-    to_a, to_b, a_took = lax.optimization_barrier((to_a, to_b, a_took))
+    to_a, a_took = lax.optimization_barrier((to_a, a_took))
     from_a = lax.ppermute(to_a, "grp", [(0, 1), (3, 2), (1, 3), (2, 0)])
-    from_b = lax.ppermute(to_b, "grp", [(1, 2), (2, 1)])
     took = [p_took] + far_took
     pieces = took + [swap(x, "blk", 1) for x in took]
     spans = ((0, cap), (cap, cap))
     own_took, to_c = partial_sums(a_took, pieces, tables_took, 2, spans, groups, cap)
     from_c = lax.ppermute(to_c, "grp", [(1, 0), (2, 3)])
-    return owner_sums([own, own_took, from_a], from_b, from_c, sub)
+    to_b, own_took = lax.optimization_barrier((to_b, own_took))
+    from_b = lax.ppermute(to_b, "grp", [(1, 2), (2, 1)])
+    return owner_sums([own, own_took, from_a], from_c, from_b, sub)
 
 
 def solution(mesh):

time: 67.5 us -> 67.7 us (level)
    ppermute x1, waiting for transfers between devices: 2.64 us -> 1.29 us  [body(): from_a = lax.ppermute(to_a, 'grp', [(0, 1), (3, 2), (1, 3), (2, 0)])]
  transfers between devices with their start and end apart: 17 -> 17, of which waited for: 6 -> 7; matrix products, arithmetic and copies ran while one was open for 0% -> 0% of each run, Pallas kernels for 36% -> 36%
where the time goes in v2:
time: 67.7 us; the launch traced here: 66.9 us
  Pallas kernels  28 us (41%)
  waiting for transfers between devices  21.3 us (31%)
  starting transfers between devices  17.4 us (26%)
    pallas_call x2, Pallas kernels, partial_sums(): pl.pallas_call(functools.partial(partial_kernel, len(pieces), spans, cap,...  19.8 us
    ppermute x1, waiting for transfers between devices, body(): from_c = lax.ppermute(to_c, 'grp', [(1, 0), (2, 3)])  10.8 us
    ppermute x12, starting transfers between devices, swap(): lax.ppermute(x, axis, [(i, i ^ d) for i in range(lax.axis_size(axis))])  10.1 us
    ppermute x12, waiting for transfers between devices, swap(): lax.ppermute(x, axis, [(i, i ^ d) for i in range(lax.axis_size(axis))])  8.98 us
    ppermute x2, starting transfers between devices, take(): return lax.ppermute(x, 'grp', takes)  4.17 us
    pallas_call x1, Pallas kernels, owner_sums(): pl.pallas_call(last_kernel, out_shape=jax.ShapeDtypeStruct((OSLOT, sub *...  4.07 us
    pallas_call x1, Pallas kernels, with_numbers(): pl.pallas_call(numbers_kernel, out_shape=jax.ShapeDtypeStruct((rf * tile...  2.3 us
    pallas_call x1, Pallas kernels, owner_sums(): pl.pallas_call(early_kernel, out_shape=table, grid_spec=pl.GridSpec(grid=...  1.82 us
  transfers between devices with their start and end apart: 17, of which 7 were waited for; matrix products, arithmetic and copies ran while one was open for 0% of the time, Pallas kernels for 36%

profile of v2, /device:TPU:0, one launch (start us, length us, event | category | flops | bytes accessed | tf_op | source)
XLA Modules:
  0.0 66.9 jit_solution(13082371324336041437)
XLA Ops:
  0.0 0.0 copy-start.1
  0.0 2.9 %collective-permute-start = (bf16[8,64,256]{2,1,0:T(8,128)(2,1)}, bf16[8,64,256]{2,1,0:T(8,128)(2,1)S(1)}, u32[]{:S(2)}, u32[]{:S(2)}) collective-permute-start(bf16[8,64,256]{2,1,0:T(8,128)(2,1)} %refs_0_.1), channel_id=1, source_target_pairs={{0,8},{4,12},{8,0},{12,4},{16,24},{20,28},{24,16},{28,20},{1,9},{5... | collective-permute-start | bytes 786440 | tf_op jit(solution)/shard_map/ppermute | solution.py:410
  2.9 2.6 %collective-permute-start.1 = (bf16[8,64,256]{2,1,0:T(8,128)(2,1)}, bf16[8,64,256]{2,1,0:T(8,128)(2,1)S(1)}, u32[]{:S(2)}, u32[]{:S(2)}) collective-permute-start(bf16[8,64,256]{2,1,0:T(8,128)(2,1)} %refs_0_.1), channel_id=1, source_target_pairs={{1,0},{3,1},{0,2},{2,3},{5,4},{7,5},{4,6},{6,7},{9,8},{11,9},{8,10... | collective-permute-start | bytes 786440 | tf_op jit(solution)/shard_map/ppermute | solution.py:425
  5.5 1.5 %collective-permute-start.2 = (bf16[8,64,256]{2,1,0:T(8,128)(2,1)}, bf16[8,64,256]{2,1,0:T(8,128)(2,1)S(1)}, u32[]{:S(2)}, u32[]{:S(2)}) collective-permute-start(bf16[8,64,256]{2,1,0:T(8,128)(2,1)} %refs_0_.1), channel_id=1, source_target_pairs={{0,16},{4,20},{8,24},{12,28},{16,0},{20,4},{24,8},{28,12},{1,17},{... | collective-permute-start | bytes 786440 | tf_op jit(solution)/shard_map/ppermute | solution.py:410
  7.1 0.5 collective-permute-start.3
  7.5 2.3 %with_numbers.1.rows_in = bf16[528,1024]{1,0:T(8,128)(2,1)} custom-call(bf16[8,64,1024]{2,1,0:T(8,128)(2,1)} %a_ref.1, s32[8,256]{1,0:T(8,128)} %route_ref.1, s32[1,256]{1,0:T(1,128)} %slot_ref.1, s32[8,16]{1,0:T(8,128)} %cols_ref.1), custom_call_target="tpu_custom_call" | custom-call | flops 1 | bytes 1 | tf_op jit(solution)/shard_map/with_numbers/pallas_call | solution.py:41
  9.8 0.0 copy-start
  9.8 1.6 %collective-permute-start.9 = (bf16[528,1024]{1,0:T(8,128)(2,1)}, bf16[528,1024]{1,0:T(8,128)(2,1)S(1)}, u32[]{:S(2)}, u32[]{:S(2)}) collective-permute-start(bf16[528,1024]{1,0:T(8,128)(2,1)} %with_numbers.1.rows_in), channel_id=1, source_target_pairs={{1,0},{3,1},{0,2},{2,3},{5,4},{7,5},{4,6},{6,7},{9,8},{11,9},{8,10... | collective-permute-start | bytes 3244040 | tf_op jit(solution)/shard_map/ppermute | solution.py:425
  11.4 0.0 collective-permute-done
  11.4 0.2 collective-permute-done.1.refs_0_
  11.7 7.2 %collective-permute-done.2 = bf16[8,64,256]{2,1,0:T(8,128)(2,1)S(1)} collective-permute-done((bf16[8,64,256]{2,1,0:T(8,128)(2,1)}, bf16[8,64,256]{2,1,0:T(8,128)(2,1)S(1)}, u32[]{:S(2)}, u32[]{:S(2)}) %collective-permute-start.2) | collective-permute-done | bytes 262176 | tf_op jit(solution)/shard_map/ppermute | solution.py:410
  18.9 0.0 collective-permute-done.3
  18.9 0.1 collective-permute-start.5
  19.0 0.0 copy-done.1
  19.0 0.5 collective-permute-start.4
  19.5 0.5 collective-permute-start.6
  20.0 1.5 %collective-permute-start.7 = (bf16[8,64,256]{2,1,0:T(8,128)(2,1)S(1)}, bf16[8,64,256]{2,1,0:T(8,128)(2,1)S(1)}, u32[]{:S(2)}, u32[]{:S(2)}) collective-permute-start(bf16[8,64,256]{2,1,0:T(8,128)(2,1)S(1)} %collective-permute-done.1.refs_0_), channel_id=1, source_target_pairs={{0,16},{4,20},{8,24},{12,28},{16,0},{20,4},{24,8},{28,12},{1,17},{... | collective-permute-start | bytes 786440 | tf_op jit(solution)/shard_map/ppermute | solution.py:410
  21.5 0.1 collective-permute-done.4.refs_2_
  21.6 1.5 %collective-permute-start.8 = (bf16[8,64,256]{2,1,0:T(8,128)(2,1)S(1)}, bf16[8,64,256]{2,1,0:T(8,128)(2,1)S(1)}, u32[]{:S(2)}, u32[]{:S(2)}) collective-permute-start(bf16[8,64,256]{2,1,0:T(8,128)(2,1)S(1)} %collective-permute-done.1.refs_0_), channel_id=1, source_target_pairs={{0,24},{4,28},{8,16},{12,20},{16,8},{20,12},{24,0},{28,4},{1,25},{... | collective-permute-start | bytes 786440 | tf_op jit(solution)/shard_map/ppermute | solution.py:410
  23.1 0.0 collective-permute-done.5.refs_3_
  23.1 0.0 copy-done
  23.1 9.9 %partial_sums.2 = (bf16[2064,128]{1,0:T(8,128)(2,1)S(1)}, bf16[2064,128]{1,0:T(8,128)(2,1)S(1)}, bf16[2064,128]{1,0:T(8,128)(2,1)S(1)}) custom-call(bf16[528,1024]{1,0:T(8,128)(2,1)S(1)} %copy-done, bf16[8,64,256]{2,1,0:T(8,128)(2,1)S(1)} %copy-done.1, bf16[24,64,256]{2,1,0:T(8,128)(2,1)S(1)} %constant_dynamic-update-slice_fusion.refs_1_, ...), custom_call_target="tpu_custom_call" | custom-call | flops 1 | bytes 1 | tf_op jit(solution)/shard_map/partial_sums/pallas_call | solution.py:225
  33.1 0.0 collective-permute-done.6.refs_1_
  33.1 0.0 collective-permute-done.7.refs_2_
  33.1 1.3 %collective-permute-done.8.refs_3_ = bf16[8,64,256]{2,1,0:T(8,128)(2,1)S(1)} collective-permute-done((bf16[8,64,256]{2,1,0:T(8,128)(2,1)S(1)}, bf16[8,64,256]{2,1,0:T(8,128)(2,1)S(1)}, u32[]{:S(2)}, u32[]{:S(2)}) %collective-permute-start.8) | collective-permute-done | bytes 262176 | tf_op jit(solution)/shard_map/ppermute | solution.py:410
  34.4 0.0 collective-permute-start.10
  34.4 0.5 collective-permute-start.11
  34.9 0.0 collective-permute-start.12
  34.9 0.5 collective-permute-start.13
  35.4 0.0 collective-permute-done.9.rows_in
  35.4 1.2 %collective-permute-start.14 = (bf16[2064,128]{1,0:T(8,128)(2,1)S(1)}, bf16[2064,128]{1,0:T(8,128)(2,1)S(1)}, u32[]{:S(2)}, u32[]{:S(2)}) collective-permute-start(bf16[2064,128]{1,0:T(8,128)(2,1)S(1)} %get-tuple-element.34), channel_id=1, source_target_pairs={{0,1},{3,2},{1,3},{2,0},{4,5},{7,6},{5,7},{6,4},{8,9},{11,10},{9,1... | collective-permute-start | bytes 1585160 | tf_op jit(solution)/shard_map/ppermute | solution.py:446
  36.6 0.0 collective-permute-done.10.refs_4_
  36.6 0.0 collective-permute-done.11.refs_5_
  36.6 0.1 collective-permute-done.12.refs_6_
  36.6 0.4 collective-permute-done.13.refs_7_
  37.0 9.9 %partial_sums.3 = (bf16[2064,128]{1,0:T(8,128)(2,1)S(1)}, bf16[2064,128]{1,0:T(8,128)(2,1)S(1)}) custom-call(bf16[528,1024]{1,0:T(8,128)(2,1)S(1)} %collective-permute-done.9.rows_in, bf16[8,64,256]{2,1,0:T(8,128)(2,1)S(1)} %collective-permute-done.1.refs_0_, bf16[8,64,256]{2,1,0:T(8,128)(2,1)S(1)} %collective-permute-done.6.refs_1_, ...), custom_call_target="tpu_custom_call" | custom-call | flops 1 | bytes 1 | tf_op jit(solution)/shard_map/partial_sums/pallas_call | solution.py:225
  46.9 1.3 %collective-permute-start.15 = (bf16[2064,128]{1,0:T(8,128)(2,1)S(1)}, bf16[2064,128]{1,0:T(8,128)(2,1)S(1)}, u32[]{:S(2)}, u32[]{:S(2)}) collective-permute-start(bf16[2064,128]{1,0:T(8,128)(2,1)S(1)} %get-tuple-element.35), channel_id=1, source_target_pairs={{1,0},{2,3},{5,4},{6,7},{9,8},{10,11},{13,12},{14,15},{17,16},{18,... | collective-permute-start | bytes 1585160 | tf_op jit(solution)/shard_map/ppermute | solution.py:451
  48.2 0.7 %collective-permute-start.16 = (bf16[2064,128]{1,0:T(8,128)(2,1)S(1)}, bf16[2064,128]{1,0:T(8,128)(2,1)S(1)}, u32[]{:S(2)}, u32[]{:S(2)}) collective-permute-start(bf16[2064,128]{1,0:T(8,128)(2,1)S(1)} %get-tuple-element.36), channel_id=1, source_target_pairs={{1,2},{2,1},{5,6},{6,5},{9,10},{10,9},{13,14},{14,13},{17,18},{18,... | collective-permute-start | bytes 1585160 | tf_op jit(solution)/shard_map/ppermute | solution.py:453
  48.9 1.3 %collective-permute-done.14.refs_2_ = bf16[2064,128]{1,0:T(8,128)(2,1)S(1)} collective-permute-done((bf16[2064,128]{1,0:T(8,128)(2,1)S(1)}, bf16[2064,128]{1,0:T(8,128)(2,1)S(1)}, u32[]{:S(2)}, u32[]{:S(2)}) %collective-permute-start.14) | collective-permute-done | bytes 528416 | tf_op jit(solution)/shard_map/ppermute | solution.py:446
  50.2 1.8 %early_sums.1.table = f32[128,32,128]{2,1,0:T(8,128)S(1)} custom-call(bf16[2064,128]{1,0:T(8,128)(2,1)S(1)} %get-tuple-element.24.refs_0_, bf16[2064,128]{1,0:T(8,128)(2,1)S(1)} %get-tuple-element.33.refs_1_, bf16[2064,128]{1,0:T(8,128)(2,1)S(1)} %collective-permute-done.14.refs_2_), custom_call_target="tpu_custom_call" | custom-call | tf_op jit(solution)/shard_map/early_sums/pallas_call | solution.py:367
  52.0 10.8 %collective-permute-done.15.from_c = bf16[2064,128]{1,0:T(8,128)(2,1)S(1)} collective-permute-done((bf16[2064,128]{1,0:T(8,128)(2,1)S(1)}, bf16[2064,128]{1,0:T(8,128)(2,1)S(1)}, u32[]{:S(2)}, u32[]{:S(2)}) %collective-permute-start.15) | collective-permute-done | bytes 528416 | tf_op jit(solution)/shard_map/ppermute | solution.py:451
  62.8 0.0 collective-permute-done.16.from_b
  62.8 4.1 %owner_sums.1 = f32[128,4096]{1,0:T(8,128)} custom-call(f32[128,32,128]{2,1,0:T(8,128)S(1)} %early_sums.1.table, bf16[2064,128]{1,0:T(8,128)(2,1)S(1)} %collective-permute-done.15.from_c, bf16[2064,128]{1,0:T(8,128)(2,1)S(1)} %collective-permute-done.16.from_b), custom_call_target="tpu_custom_call" | custom-call | tf_op jit(solution)/shard_map/owner_sums/pallas_call | solution.py:386
  (3 shorter events, 0.1 us)
Async XLA Ops:
  0.0 19.0 %copy-start.1 = (bf16[8,64,256]{2,1,0:T(8,128)(2,1)S(1)}, bf16[8,64,256]{2,1,0:T(8,128)(2,1)}, u32[]{:S(2)}) copy-start(bf16[8,64,256]{2,1,0:T(8,128)(2,1)} %refs_0_.1) | copy-start | bytes 786436
  0.0 11.4 %collective-permute-start = (bf16[8,64,256]{2,1,0:T(8,128)(2,1)}, bf16[8,64,256]{2,1,0:T(8,128)(2,1)S(1)}, u32[]{:S(2)}, u32[]{:S(2)}) collective-permute-start(bf16[8,64,256]{2,1,0:T(8,128)(2,1)} %refs_0_.1), channel_id=1, source_target_pairs={{0,8},{4,12},{8,0},{12,4},{16,24},{20,28},{24,16},{28,20},{1,9},{5... | collective-permute-start | bytes 786440 | tf_op jit(solution)/shard_map/ppermute | solution.py:410
  2.9 8.7 %collective-permute-start.1 = (bf16[8,64,256]{2,1,0:T(8,128)(2,1)}, bf16[8,64,256]{2,1,0:T(8,128)(2,1)S(1)}, u32[]{:S(2)}, u32[]{:S(2)}) collective-permute-start(bf16[8,64,256]{2,1,0:T(8,128)(2,1)} %refs_0_.1), channel_id=1, source_target_pairs={{1,0},{3,1},{0,2},{2,3},{5,4},{7,5},{4,6},{6,7},{9,8},{11,9},{8,10... | collective-permute-start | bytes 786440 | tf_op jit(solution)/shard_map/ppermute | solution.py:425
  5.5 13.3 %collective-permute-start.2 = (bf16[8,64,256]{2,1,0:T(8,128)(2,1)}, bf16[8,64,256]{2,1,0:T(8,128)(2,1)S(1)}, u32[]{:S(2)}, u32[]{:S(2)}) collective-permute-start(bf16[8,64,256]{2,1,0:T(8,128)(2,1)} %refs_0_.1), channel_id=1, source_target_pairs={{0,16},{4,20},{8,24},{12,28},{16,0},{20,4},{24,8},{28,12},{1,17},{... | collective-permute-start | bytes 786440 | tf_op jit(solution)/shard_map/ppermute | solution.py:410
  7.1 11.8 %collective-permute-start.3 = (bf16[8,64,256]{2,1,0:T(8,128)(2,1)}, bf16[8,64,256]{2,1,0:T(8,128)(2,1)S(1)}, u32[]{:S(2)}, u32[]{:S(2)}) collective-permute-start(bf16[8,64,256]{2,1,0:T(8,128)(2,1)} %refs_0_.1), channel_id=1, source_target_pairs={{0,24},{4,28},{8,16},{12,20},{16,8},{20,12},{24,0},{28,4},{1,25},{... | collective-permute-start | bytes 786440 | tf_op jit(solution)/shard_map/ppermute | solution.py:410
  9.8 13.3 %copy-start = (bf16[528,1024]{1,0:T(8,128)(2,1)S(1)}, bf16[528,1024]{1,0:T(8,128)(2,1)}, u32[]{:S(2)}) copy-start(bf16[528,1024]{1,0:T(8,128)(2,1)} %with_numbers.1.rows_in) | copy-start | bytes 3244036
  9.8 25.5 %collective-permute-start.9 = (bf16[528,1024]{1,0:T(8,128)(2,1)}, bf16[528,1024]{1,0:T(8,128)(2,1)S(1)}, u32[]{:S(2)}, u32[]{:S(2)}) collective-permute-start(bf16[528,1024]{1,0:T(8,128)(2,1)} %with_numbers.1.rows_in), channel_id=1, source_target_pairs={{1,0},{3,1},{0,2},{2,3},{5,4},{7,5},{4,6},{6,7},{9,8},{11,9},{8,10... | collective-permute-start | bytes 3244040 | tf_op jit(solution)/shard_map/ppermute | solution.py:425
  18.9 4.2 %collective-permute-start.5 = (bf16[24,64,256]{2,1,0:T(8,128)(2,1)S(1)}, bf16[24,64,256]{2,1,0:T(8,128)(2,1)S(1)}, u32[]{:S(2)}, u32[]{:S(2)}) collective-permute-start(bf16[24,64,256]{2,1,0:T(8,128)(2,1)S(1)} %constant_dynamic-update-slice_fusion.refs_1_), channel_id=1, source_target_pairs={{0,4},{4,0},{8,12},{12,8},{16,20},{20,16},{24,28},{28,24},{1,5},{5... | collective-permute-start | bytes 2359304 | tf_op jit(solution)/shard_map/ppermute | solution.py:410
  19.0 2.6 %collective-permute-start.4 = (bf16[8,64,256]{2,1,0:T(8,128)(2,1)S(1)}, bf16[8,64,256]{2,1,0:T(8,128)(2,1)S(1)}, u32[]{:S(2)}, u32[]{:S(2)}) collective-permute-start(bf16[8,64,256]{2,1,0:T(8,128)(2,1)S(1)} %copy-done.1), channel_id=1, source_target_pairs={{0,4},{4,0},{8,12},{12,8},{16,20},{20,16},{24,28},{28,24},{1,5},{5... | collective-permute-start | bytes 786440 | tf_op jit(solution)/shard_map/ppermute | solution.py:410
  19.5 13.6 %collective-permute-start.6 = (bf16[8,64,256]{2,1,0:T(8,128)(2,1)S(1)}, bf16[8,64,256]{2,1,0:T(8,128)(2,1)S(1)}, u32[]{:S(2)}, u32[]{:S(2)}) collective-permute-start(bf16[8,64,256]{2,1,0:T(8,128)(2,1)S(1)} %collective-permute-done.1.refs_0_), channel_id=1, source_target_pairs={{0,8},{4,12},{8,0},{12,4},{16,24},{20,28},{24,16},{28,20},{1,9},{5... | collective-permute-start | bytes 786440 | tf_op jit(solution)/shard_map/ppermute | solution.py:410
  20.0 13.1 %collective-permute-start.7 = (bf16[8,64,256]{2,1,0:T(8,128)(2,1)S(1)}, bf16[8,64,256]{2,1,0:T(8,128)(2,1)S(1)}, u32[]{:S(2)}, u32[]{:S(2)}) collective-permute-start(bf16[8,64,256]{2,1,0:T(8,128)(2,1)S(1)} %collective-permute-done.1.refs_0_), channel_id=1, source_target_pairs={{0,16},{4,20},{8,24},{12,28},{16,0},{20,4},{24,8},{28,12},{1,17},{... | collective-permute-start | bytes 786440 | tf_op jit(solution)/shard_map/ppermute | solution.py:410
  21.6 12.7 %collective-permute-start.8 = (bf16[8,64,256]{2,1,0:T(8,128)(2,1)S(1)}, bf16[8,64,256]{2,1,0:T(8,128)(2,1)S(1)}, u32[]{:S(2)}, u32[]{:S(2)}) collective-permute-start(bf16[8,64,256]{2,1,0:T(8,128)(2,1)S(1)} %collective-permute-done.1.refs_0_), channel_id=1, source_target_pairs={{0,24},{4,28},{8,16},{12,20},{16,8},{20,12},{24,0},{28,4},{1,25},{... | collective-permute-start | bytes 786440 | tf_op jit(solution)/shard_map/ppermute | solution.py:410
  34.4 2.2 %collective-permute-start.10 = (bf16[8,64,256]{2,1,0:T(8,128)(2,1)S(1)}, bf16[8,64,256]{2,1,0:T(8,128)(2,1)S(1)}, u32[]{:S(2)}, u32[]{:S(2)}) collective-permute-start(bf16[8,64,256]{2,1,0:T(8,128)(2,1)S(1)} %collective-permute-done.1.refs_0_), channel_id=1, source_target_pairs={{0,4},{4,0},{8,12},{12,8},{16,20},{20,16},{24,28},{28,24},{1,5},{5... | collective-permute-start | bytes 786440 | tf_op jit(solution)/shard_map/ppermute | solution.py:410
  34.4 2.2 %collective-permute-start.11 = (bf16[8,64,256]{2,1,0:T(8,128)(2,1)S(1)}, bf16[8,64,256]{2,1,0:T(8,128)(2,1)S(1)}, u32[]{:S(2)}, u32[]{:S(2)}) collective-permute-start(bf16[8,64,256]{2,1,0:T(8,128)(2,1)S(1)} %collective-permute-done.6.refs_1_), channel_id=1, source_target_pairs={{0,4},{4,0},{8,12},{12,8},{16,20},{20,16},{24,28},{28,24},{1,5},{5... | collective-permute-start | bytes 786440 | tf_op jit(solution)/shard_map/ppermute | solution.py:410
  34.9 1.8 %collective-permute-start.12 = (bf16[8,64,256]{2,1,0:T(8,128)(2,1)S(1)}, bf16[8,64,256]{2,1,0:T(8,128)(2,1)S(1)}, u32[]{:S(2)}, u32[]{:S(2)}) collective-permute-start(bf16[8,64,256]{2,1,0:T(8,128)(2,1)S(1)} %collective-permute-done.7.refs_2_), channel_id=1, source_target_pairs={{0,4},{4,0},{8,12},{12,8},{16,20},{20,16},{24,28},{28,24},{1,5},{5... | collective-permute-start | bytes 786440 | tf_op jit(solution)/shard_map/ppermute | solution.py:410
  34.9 2.1 %collective-permute-start.13 = (bf16[8,64,256]{2,1,0:T(8,128)(2,1)S(1)}, bf16[8,64,256]{2,1,0:T(8,128)(2,1)S(1)}, u32[]{:S(2)}, u32[]{:S(2)}) collective-permute-start(bf16[8,64,256]{2,1,0:T(8,128)(2,1)S(1)} %collective-permute-done.8.refs_3_), channel_id=1, source_target_pairs={{0,4},{4,0},{8,12},{12,8},{16,20},{20,16},{24,28},{28,24},{1,5},{5... | collective-permute-start | bytes 786440 | tf_op jit(solution)/shard_map/ppermute | solution.py:410
  35.4 14.8 %collective-permute-start.14 = (bf16[2064,128]{1,0:T(8,128)(2,1)S(1)}, bf16[2064,128]{1,0:T(8,128)(2,1)S(1)}, u32[]{:S(2)}, u32[]{:S(2)}) collective-permute-start(bf16[2064,128]{1,0:T(8,128)(2,1)S(1)} %get-tuple-element.34), channel_id=1, source_target_pairs={{0,1},{3,2},{1,3},{2,0},{4,5},{7,6},{5,7},{6,4},{8,9},{11,10},{9,1... | collective-permute-start | bytes 1585160 | tf_op jit(solution)/shard_map/ppermute | solution.py:446
  46.9 15.9 %collective-permute-start.15 = (bf16[2064,128]{1,0:T(8,128)(2,1)S(1)}, bf16[2064,128]{1,0:T(8,128)(2,1)S(1)}, u32[]{:S(2)}, u32[]{:S(2)}) collective-permute-start(bf16[2064,128]{1,0:T(8,128)(2,1)S(1)} %get-tuple-element.35), channel_id=1, source_target_pairs={{1,0},{2,3},{5,4},{6,7},{9,8},{10,11},{13,12},{14,15},{17,16},{18,... | collective-permute-start | bytes 1585160 | tf_op jit(solution)/shard_map/ppermute | solution.py:451
  48.2 14.6 %collective-permute-start.16 = (bf16[2064,128]{1,0:T(8,128)(2,1)S(1)}, bf16[2064,128]{1,0:T(8,128)(2,1)S(1)}, u32[]{:S(2)}, u32[]{:S(2)}) collective-permute-start(bf16[2064,128]{1,0:T(8,128)(2,1)S(1)} %get-tuple-element.36), channel_id=1, source_target_pairs={{1,2},{2,1},{5,6},{6,5},{9,10},{10,9},{13,14},{14,13},{17,18},{18,... | collective-permute-start | bytes 1585160 | tf_op jit(solution)/shard_map/ppermute | solution.py:453

commit v3 on v0

--- a/solution.py
+++ b/solution.py
@@ -294,17 +294,15 @@
     lax.fori_loop(0, n_out // chunk, merge, 0)
 
 
-def last_kernel(table, from_b, from_c, out_ref, acc, late, rows_buf, vmem_names, smem_names, sems):
+def last_kernel(names, table, from_b, from_c, out_ref, acc, late, rows_buf, sems):
     n_out, sub = acc.shape[:2]
-    cap = (late.shape[0] - NAME_ROWS) // sub
+    cap = late.shape[0] // sub
     me = lax.axis_index("grp")
     at = me * cap
-    row, lane = lax.div(at, jnp.int32(LANES)), lax.rem(at, jnp.int32(LANES))
-    parts = (sems.shape[0] - 2) // 3
+    parts = sems.shape[0] // 3
 
     def late_copies(table_in):
-        spans = [pl.ds(cap * sub, NAME_ROWS)]
-        spans += [pl.ds(n * (cap // parts) * sub, cap // parts * sub) for n in range(parts)]
+        spans = [pl.ds(n * (cap // parts) * sub, cap // parts * sub) for n in range(parts)]
         return [
             pltpu.make_async_copy(table_in.at[span], late.at[span], sems.at[n]) for n, span in enumerate(spans)
         ]
@@ -324,20 +322,15 @@
     height = n_out // parts
     blocks = [pl.ds(n * height, height) for n in range(parts)]
     fills = [
-        pltpu.make_async_copy(table.at[span], acc.at[span], sems.at[1 + parts + n]) for n, span in enumerate(blocks)
+        pltpu.make_async_copy(table.at[span], acc.at[span], sems.at[parts + n]) for n, span in enumerate(blocks)
     ]
     for copy in fills:
         copy.start()
-    waiting = late_copies(from_b)
-    waiting.pop(0).wait()
-    vmem_names[...] = late[pl.ds(cap * sub, NAME_ROWS), :].astype(jnp.float32).astype(jnp.int32)
-    copy = pltpu.make_async_copy(vmem_names, smem_names, sems.at[1 + 2 * parts])
-    copy.start()
-    for other in waiting + fills + [copy]:
-        other.wait()
+    for copy in late_copies(from_b) + fills:
+        copy.wait()
 
     def add(c, carry):
-        acc[smem_names[row, lane + c]] += late[pl.ds(pl.multiple_of(c * sub, sub), sub), :].astype(jnp.float32)
+        acc[names[0, at + c]] += late[pl.ds(pl.multiple_of(c * sub, sub), sub), :].astype(jnp.float32)
         return carry
 
     lax.fori_loop(0, cap, add, 0, unroll=4)
@@ -352,13 +345,13 @@
     copies = []
     for n, rows in enumerate(blocks):
         lax.fori_loop(n * height // 8, (n + 1) * height // 8, emit, 0)
-        copies.append(pltpu.make_async_copy(rows_buf.at[rows], out_ref.at[rows], sems.at[2 + 2 * parts + n]))
+        copies.append(pltpu.make_async_copy(rows_buf.at[rows], out_ref.at[rows], sems.at[2 * parts + n]))
         copies[-1].start()
     for copy in copies:
         copy.wait()
 
 
-def owner_sums(tables, from_b, from_c, sub):
+def owner_sums(tables, last_names, from_b, from_c, sub):
     def whole(x):
         return pl.BlockSpec(x.shape, lambda i: (0,) * len(x.shape))
 
@@ -386,24 +379,23 @@
     return pl.pallas_call(
         last_kernel,
         out_shape=jax.ShapeDtypeStruct((OSLOT, sub * LANES), jnp.float32),
-        grid_spec=pl.GridSpec(
+        grid_spec=pltpu.PrefetchScalarGridSpec(
+            num_scalar_prefetch=1,
             grid=(1,),
             in_specs=[pl.BlockSpec(memory_space=pl.ANY)] * 3,
             out_specs=pl.BlockSpec(memory_space=pl.ANY),
             scratch_shapes=[
                 pltpu.VMEM(table.shape, jnp.float32),
-                pltpu.VMEM(from_b.shape, jnp.bfloat16),
+                pltpu.VMEM((from_b.shape[0] - NAME_ROWS, LANES), jnp.bfloat16),
                 pltpu.VMEM((OSLOT, sub * LANES), jnp.float32),
-                pltpu.VMEM(names, jnp.int32),
-                pltpu.SMEM(names, jnp.int32),
-                pltpu.SemaphoreType.DMA((2 + 3 * 4,)),
+                pltpu.SemaphoreType.DMA((3 * 4,)),
             ],
         ),
         compiler_params=pltpu.CompilerParams(
             dimension_semantics=("arbitrary",), vmem_limit_bytes=20 * 1024 * 1024
         ),
         name="owner_sums",
-    )(early, from_b, from_c)
+    )(last_names, early, from_b, from_c)
 
 
 def swap(x, axis, d):
@@ -450,7 +442,8 @@
     spans = ((0, cap), (cap, cap))
     own_took, to_c = partial_sums(a_took, pieces, tables_took, 2, spans, groups, cap)
     from_c = lax.ppermute(to_c, "grp", [(1, 0), (2, 3)])
-    return owner_sums([own, own_took, from_a], from_b, from_c, sub)
+    last_names = swap(out_slot, "grp", groups - 1)
+    return owner_sums([own, own_took, from_a], last_names, from_b, from_c, sub)
 
 
 def solution(mesh):

time: 67.5 us -> 67.4 us (level)
  starting transfers between devices: 17.4 us -> 19.9 us
  waiting for transfers between devices: 21.7 us -> 19.2 us
    ppermute x1, waiting for transfers between devices: 2.64 us -> 0.1 us  [body(): from_a = lax.ppermute(to_a, 'grp', [(0, 1), (3, 2), (1, 3), (2, 0)])]
    ppermute x12 -> x13, starting transfers between devices: 10.1 us -> 12.6 us  [swap(): lax.ppermute(x, axis, [(i, i ^ d) for i in range(lax.axis_size(axis))])]
    ppermute x12 -> x13, waiting for transfers between devices: 8.58 us -> 9.57 us  [swap(): lax.ppermute(x, axis, [(i, i ^ d) for i in range(lax.axis_size(axis))])]
    ppermute x1, waiting for transfers between devices: 10.3 us -> 9.32 us  [body(): from_c = lax.ppermute(to_c, 'grp', [(1, 0), (2, 3)])]
  transfers between devices with their start and end apart: 17 -> 18, of which waited for: 6 -> 7; matrix products, arithmetic and copies ran while one was open for 0% -> 0% of each run, Pallas kernels for 36% -> 36%
where the time goes in v3:
time: 67.4 us; the launch traced here: 67.2 us
  Pallas kernels  27.8 us (41%)
  starting transfers between devices  19.9 us (30%)
  waiting for transfers between devices  19.2 us (28%)
    pallas_call x2, Pallas kernels, partial_sums(): pl.pallas_call(functools.partial(partial_kernel, len(pieces), spans, cap,...  19.8 us
    ppermute x13, starting transfers between devices, swap(): lax.ppermute(x, axis, [(i, i ^ d) for i in range(lax.axis_size(axis))])  12.6 us
    ppermute x13, waiting for transfers between devices, swap(): lax.ppermute(x, axis, [(i, i ^ d) for i in range(lax.axis_size(axis))])  9.57 us
    ppermute x1, waiting for transfers between devices, body(): from_c = lax.ppermute(to_c, 'grp', [(1, 0), (2, 3)])  9.32 us
    ppermute x2, starting transfers between devices, take(): return lax.ppermute(x, 'grp', takes)  4.17 us
    pallas_call x1, Pallas kernels, owner_sums(): pl.pallas_call(last_kernel, out_shape=jax.ShapeDtypeStruct((OSLOT, sub *...  3.91 us
    pallas_call x1, Pallas kernels, with_numbers(): pl.pallas_call(numbers_kernel, out_shape=jax.ShapeDtypeStruct((rf * tile...  2.3 us
    pallas_call x1, Pallas kernels, owner_sums(): pl.pallas_call(early_kernel, out_shape=table, grid_spec=pl.GridSpec(grid=...  1.82 us
  transfers between devices with their start and end apart: 18, of which 7 were waited for; matrix products, arithmetic and copies ran while one was open for 0% of the time, Pallas kernels for 36%

profile of v3, /device:TPU:0, one launch (start us, length us, event | category | flops | bytes accessed | tf_op | source)
XLA Modules:
  0.0 67.2 jit_solution(10910430106704477513)
XLA Ops:
  0.0 0.0 copy-start.1
  0.0 2.9 %collective-permute-start.1 = (bf16[8,64,256]{2,1,0:T(8,128)(2,1)}, bf16[8,64,256]{2,1,0:T(8,128)(2,1)S(1)}, u32[]{:S(2)}, u32[]{:S(2)}) collective-permute-start(bf16[8,64,256]{2,1,0:T(8,128)(2,1)} %refs_0_.1), channel_id=1, source_target_pairs={{0,8},{4,12},{8,0},{12,4},{16,24},{20,28},{24,16},{28,20},{1,9},{5... | collective-permute-start | bytes 786440 | tf_op jit(solution)/shard_map/ppermute | solution.py:402
  2.9 2.6 %collective-permute-start.2 = (bf16[8,64,256]{2,1,0:T(8,128)(2,1)}, bf16[8,64,256]{2,1,0:T(8,128)(2,1)S(1)}, u32[]{:S(2)}, u32[]{:S(2)}) collective-permute-start(bf16[8,64,256]{2,1,0:T(8,128)(2,1)} %refs_0_.1), channel_id=1, source_target_pairs={{1,0},{3,1},{0,2},{2,3},{5,4},{7,5},{4,6},{6,7},{9,8},{11,9},{8,10... | collective-permute-start | bytes 786440 | tf_op jit(solution)/shard_map/ppermute | solution.py:417
  5.5 1.5 %collective-permute-start.3 = (bf16[8,64,256]{2,1,0:T(8,128)(2,1)}, bf16[8,64,256]{2,1,0:T(8,128)(2,1)S(1)}, u32[]{:S(2)}, u32[]{:S(2)}) collective-permute-start(bf16[8,64,256]{2,1,0:T(8,128)(2,1)} %refs_0_.1), channel_id=1, source_target_pairs={{0,16},{4,20},{8,24},{12,28},{16,0},{20,4},{24,8},{28,12},{1,17},{... | collective-permute-start | bytes 786440 | tf_op jit(solution)/shard_map/ppermute | solution.py:402
  7.1 0.5 collective-permute-start.4
  7.5 2.3 %with_numbers.1.rows_in = bf16[528,1024]{1,0:T(8,128)(2,1)} custom-call(bf16[8,64,1024]{2,1,0:T(8,128)(2,1)} %a_ref.1, s32[8,256]{1,0:T(8,128)} %route_ref.1, s32[1,256]{1,0:T(1,128)} %slot_ref.1, s32[8,16]{1,0:T(8,128)} %cols_ref.1), custom_call_target="tpu_custom_call" | custom-call | flops 1 | bytes 1 | tf_op jit(solution)/shard_map/with_numbers/pallas_call | solution.py:41
  9.8 0.0 copy-start
  9.8 1.6 %collective-permute-start.10 = (bf16[528,1024]{1,0:T(8,128)(2,1)}, bf16[528,1024]{1,0:T(8,128)(2,1)S(1)}, u32[]{:S(2)}, u32[]{:S(2)}) collective-permute-start(bf16[528,1024]{1,0:T(8,128)(2,1)} %with_numbers.1.rows_in), channel_id=1, source_target_pairs={{1,0},{3,1},{0,2},{2,3},{5,4},{7,5},{4,6},{6,7},{9,8},{11,9},{8,10... | collective-permute-start | bytes 3244040 | tf_op jit(solution)/shard_map/ppermute | solution.py:417
  11.4 0.0 collective-permute-done.1
  11.4 0.2 collective-permute-done.2.refs_0_
  11.7 7.2 %collective-permute-done.3 = bf16[8,64,256]{2,1,0:T(8,128)(2,1)S(1)} collective-permute-done((bf16[8,64,256]{2,1,0:T(8,128)(2,1)}, bf16[8,64,256]{2,1,0:T(8,128)(2,1)S(1)}, u32[]{:S(2)}, u32[]{:S(2)}) %collective-permute-start.3) | collective-permute-done | bytes 262176 | tf_op jit(solution)/shard_map/ppermute | solution.py:402
  18.9 0.0 collective-permute-done.4
  18.9 0.1 collective-permute-start.6
  19.0 0.0 copy-done.1
  19.0 0.5 collective-permute-start.5
  19.5 0.5 collective-permute-start.7
  20.0 1.5 %collective-permute-start.8 = (bf16[8,64,256]{2,1,0:T(8,128)(2,1)S(1)}, bf16[8,64,256]{2,1,0:T(8,128)(2,1)S(1)}, u32[]{:S(2)}, u32[]{:S(2)}) collective-permute-start(bf16[8,64,256]{2,1,0:T(8,128)(2,1)S(1)} %collective-permute-done.2.refs_0_), channel_id=1, source_target_pairs={{0,16},{4,20},{8,24},{12,28},{16,0},{20,4},{24,8},{28,12},{1,17},{... | collective-permute-start | bytes 786440 | tf_op jit(solution)/shard_map/ppermute | solution.py:402
  21.5 0.1 collective-permute-done.5.refs_2_
  21.6 1.5 %collective-permute-start.9 = (bf16[8,64,256]{2,1,0:T(8,128)(2,1)S(1)}, bf16[8,64,256]{2,1,0:T(8,128)(2,1)S(1)}, u32[]{:S(2)}, u32[]{:S(2)}) collective-permute-start(bf16[8,64,256]{2,1,0:T(8,128)(2,1)S(1)} %collective-permute-done.2.refs_0_), channel_id=1, source_target_pairs={{0,24},{4,28},{8,16},{12,20},{16,8},{20,12},{24,0},{28,4},{1,25},{... | collective-permute-start | bytes 786440 | tf_op jit(solution)/shard_map/ppermute | solution.py:402
  23.1 0.0 collective-permute-done.6.refs_3_
  23.1 0.0 copy-done
  23.1 9.9 %partial_sums.2 = (bf16[2064,128]{1,0:T(8,128)(2,1)S(1)}, bf16[2064,128]{1,0:T(8,128)(2,1)S(1)}, bf16[2064,128]{1,0:T(8,128)(2,1)S(1)}) custom-call(bf16[528,1024]{1,0:T(8,128)(2,1)S(1)} %copy-done, bf16[8,64,256]{2,1,0:T(8,128)(2,1)S(1)} %copy-done.1, bf16[24,64,256]{2,1,0:T(8,128)(2,1)S(1)} %constant_dynamic-update-slice_fusion.refs_1_, ...), custom_call_target="tpu_custom_call" | custom-call | flops 1 | bytes 1 | tf_op jit(solution)/shard_map/partial_sums/pallas_call | solution.py:225
  33.0 0.0 copy-start.2
  33.1 0.0 collective-permute-done.7.refs_1_
  33.1 0.0 collective-permute-done.8.refs_2_
  33.1 1.3 %collective-permute-done.9.refs_3_ = bf16[8,64,256]{2,1,0:T(8,128)(2,1)S(1)} collective-permute-done((bf16[8,64,256]{2,1,0:T(8,128)(2,1)S(1)}, bf16[8,64,256]{2,1,0:T(8,128)(2,1)S(1)}, u32[]{:S(2)}, u32[]{:S(2)}) %collective-permute-start.9) | collective-permute-done | bytes 262176 | tf_op jit(solution)/shard_map/ppermute | solution.py:402
  34.4 0.0 collective-permute-start.11
  34.4 0.5 collective-permute-start.12
  34.9 0.0 collective-permute-start.13
  34.9 0.5 collective-permute-start.14
  35.4 0.0 collective-permute-done.10.rows_in
  35.4 1.2 %collective-permute-start.15 = (bf16[2064,128]{1,0:T(8,128)(2,1)S(1)}, bf16[2064,128]{1,0:T(8,128)(2,1)S(1)}, u32[]{:S(2)}, u32[]{:S(2)}) collective-permute-start(bf16[2064,128]{1,0:T(8,128)(2,1)S(1)} %get-tuple-element.32), channel_id=1, source_target_pairs={{0,1},{3,2},{1,3},{2,0},{4,5},{7,6},{5,7},{6,4},{8,9},{11,10},{9,1... | collective-permute-start | bytes 1585160 | tf_op jit(solution)/shard_map/ppermute | solution.py:438
  36.6 0.0 collective-permute-done.11.refs_4_
  36.6 0.7 %collective-permute-start.16 = (bf16[2064,128]{1,0:T(8,128)(2,1)S(1)}, bf16[2064,128]{1,0:T(8,128)(2,1)S(1)}, u32[]{:S(2)}, u32[]{:S(2)}) collective-permute-start(bf16[2064,128]{1,0:T(8,128)(2,1)S(1)} %get-tuple-element.33), channel_id=1, source_target_pairs={{1,2},{2,1},{5,6},{6,5},{9,10},{10,9},{13,14},{14,13},{17,18},{18,... | collective-permute-start | bytes 1585160 | tf_op jit(solution)/shard_map/ppermute | solution.py:439
  37.3 0.0 collective-permute-done.12.refs_5_
  37.3 0.0 collective-permute-done.13.refs_6_
  37.3 0.0 collective-permute-done.14.refs_7_
  37.3 9.9 %partial_sums.3 = (bf16[2064,128]{1,0:T(8,128)(2,1)S(1)}, bf16[2064,128]{1,0:T(8,128)(2,1)S(1)}) custom-call(bf16[528,1024]{1,0:T(8,128)(2,1)S(1)} %collective-permute-done.10.rows_in, bf16[8,64,256]{2,1,0:T(8,128)(2,1)S(1)} %collective-permute-done.2.refs_0_, bf16[8,64,256]{2,1,0:T(8,128)(2,1)S(1)} %collective-permute-done.7.refs_1_, ...), custom_call_target="tpu_custom_call" | custom-call | flops 1 | bytes 1 | tf_op jit(solution)/shard_map/partial_sums/pallas_call | solution.py:225
  47.2 1.3 %collective-permute-start.17 = (bf16[2064,128]{1,0:T(8,128)(2,1)S(1)}, bf16[2064,128]{1,0:T(8,128)(2,1)S(1)}, u32[]{:S(2)}, u32[]{:S(2)}) collective-permute-start(bf16[2064,128]{1,0:T(8,128)(2,1)S(1)} %get-tuple-element.34), channel_id=1, source_target_pairs={{1,0},{2,3},{5,4},{6,7},{9,8},{10,11},{13,12},{14,15},{17,16},{18,... | collective-permute-start | bytes 1585160 | tf_op jit(solution)/shard_map/ppermute | solution.py:444
  48.5 0.0 copy-done.2
  48.5 2.5 %collective-permute-start = (s32[1,256]{1,0:T(1,128)S(1)}, s32[1,256]{1,0:T(1,128)S(1)}, u32[]{:S(2)}, u32[]{:S(2)}) collective-permute-start(s32[1,256]{1,0:T(1,128)S(1)} %copy-done.2), channel_id=1, source_target_pairs={{0,3},{1,2},{2,1},{3,0},{4,7},{5,6},{6,5},{7,4},{8,11},{9,10},{10,... | collective-permute-start | bytes 3080 | tf_op jit(solution)/shard_map/ppermute | solution.py:402
  51.1 0.1 collective-permute-done.15.refs_2_
  51.2 1.8 %early_sums.1.table = f32[128,32,128]{2,1,0:T(8,128)S(1)} custom-call(bf16[2064,128]{1,0:T(8,128)(2,1)S(1)} %get-tuple-element.23.refs_0_, bf16[2064,128]{1,0:T(8,128)(2,1)S(1)} %get-tuple-element.31.refs_1_, bf16[2064,128]{1,0:T(8,128)(2,1)S(1)} %collective-permute-done.15.refs_2_), custom_call_target="tpu_custom_call" | custom-call | tf_op jit(solution)/shard_map/early_sums/pallas_call | solution.py:360
  53.0 1.0 %collective-permute-done.names = s32[1,256]{1,0:T(1,128)S(1)} collective-permute-done((s32[1,256]{1,0:T(1,128)S(1)}, s32[1,256]{1,0:T(1,128)S(1)}, u32[]{:S(2)}, u32[]{:S(2)}) %collective-permute-start) | collective-permute-done | bytes 1056 | tf_op jit(solution)/shard_map/ppermute | solution.py:402
  54.0 0.0 collective-permute-done.16.from_b
  54.0 9.3 %collective-permute-done.17.from_c = bf16[2064,128]{1,0:T(8,128)(2,1)S(1)} collective-permute-done((bf16[2064,128]{1,0:T(8,128)(2,1)S(1)}, bf16[2064,128]{1,0:T(8,128)(2,1)S(1)}, u32[]{:S(2)}, u32[]{:S(2)}) %collective-permute-start.17) | collective-permute-done | bytes 528416 | tf_op jit(solution)/shard_map/ppermute | solution.py:444
  63.3 3.9 %owner_sums.1 = f32[128,4096]{1,0:T(8,128)} custom-call(s32[1,256]{1,0:T(1,128)S(1)} %collective-permute-done.names, f32[128,32,128]{2,1,0:T(8,128)S(1)} %early_sums.1.table, bf16[2064,128]{1,0:T(8,128)(2,1)S(1)} %collective-permute-done.16.from_b, bf16[2064,128]{1,0:T(8,128)(2,1)S(1)} %collective-permute-done.17.from_c), custom_call_target="tpu_custom_call" | custom-call | tf_op jit(solution)/shard_map/owner_sums/pallas_call | solution.py:379
  (3 shorter events, 0.1 us)
Async XLA Ops:
  0.0 19.0 %copy-start.1 = (bf16[8,64,256]{2,1,0:T(8,128)(2,1)S(1)}, bf16[8,64,256]{2,1,0:T(8,128)(2,1)}, u32[]{:S(2)}) copy-start(bf16[8,64,256]{2,1,0:T(8,128)(2,1)} %refs_0_.1) | copy-start | bytes 786436
  0.0 11.4 %collective-permute-start.1 = (bf16[8,64,256]{2,1,0:T(8,128)(2,1)}, bf16[8,64,256]{2,1,0:T(8,128)(2,1)S(1)}, u32[]{:S(2)}, u32[]{:S(2)}) collective-permute-start(bf16[8,64,256]{2,1,0:T(8,128)(2,1)} %refs_0_.1), channel_id=1, source_target_pairs={{0,8},{4,12},{8,0},{12,4},{16,24},{20,28},{24,16},{28,20},{1,9},{5... | collective-permute-start | bytes 786440 | tf_op jit(solution)/shard_map/ppermute | solution.py:402
  2.9 8.7 %collective-permute-start.2 = (bf16[8,64,256]{2,1,0:T(8,128)(2,1)}, bf16[8,64,256]{2,1,0:T(8,128)(2,1)S(1)}, u32[]{:S(2)}, u32[]{:S(2)}) collective-permute-start(bf16[8,64,256]{2,1,0:T(8,128)(2,1)} %refs_0_.1), channel_id=1, source_target_pairs={{1,0},{3,1},{0,2},{2,3},{5,4},{7,5},{4,6},{6,7},{9,8},{11,9},{8,10... | collective-permute-start | bytes 786440 | tf_op jit(solution)/shard_map/ppermute | solution.py:417
  5.5 13.3 %collective-permute-start.3 = (bf16[8,64,256]{2,1,0:T(8,128)(2,1)}, bf16[8,64,256]{2,1,0:T(8,128)(2,1)S(1)}, u32[]{:S(2)}, u32[]{:S(2)}) collective-permute-start(bf16[8,64,256]{2,1,0:T(8,128)(2,1)} %refs_0_.1), channel_id=1, source_target_pairs={{0,16},{4,20},{8,24},{12,28},{16,0},{20,4},{24,8},{28,12},{1,17},{... | collective-permute-start | bytes 786440 | tf_op jit(solution)/shard_map/ppermute | solution.py:402
  7.1 11.8 %collective-permute-start.4 = (bf16[8,64,256]{2,1,0:T(8,128)(2,1)}, bf16[8,64,256]{2,1,0:T(8,128)(2,1)S(1)}, u32[]{:S(2)}, u32[]{:S(2)}) collective-permute-start(bf16[8,64,256]{2,1,0:T(8,128)(2,1)} %refs_0_.1), channel_id=1, source_target_pairs={{0,24},{4,28},{8,16},{12,20},{16,8},{20,12},{24,0},{28,4},{1,25},{... | collective-permute-start | bytes 786440 | tf_op jit(solution)/shard_map/ppermute | solution.py:402
  9.8 13.3 %copy-start = (bf16[528,1024]{1,0:T(8,128)(2,1)S(1)}, bf16[528,1024]{1,0:T(8,128)(2,1)}, u32[]{:S(2)}) copy-start(bf16[528,1024]{1,0:T(8,128)(2,1)} %with_numbers.1.rows_in) | copy-start | bytes 3244036
  9.8 25.5 %collective-permute-start.10 = (bf16[528,1024]{1,0:T(8,128)(2,1)}, bf16[528,1024]{1,0:T(8,128)(2,1)S(1)}, u32[]{:S(2)}, u32[]{:S(2)}) collective-permute-start(bf16[528,1024]{1,0:T(8,128)(2,1)} %with_numbers.1.rows_in), channel_id=1, source_target_pairs={{1,0},{3,1},{0,2},{2,3},{5,4},{7,5},{4,6},{6,7},{9,8},{11,9},{8,10... | collective-permute-start | bytes 3244040 | tf_op jit(solution)/shard_map/ppermute | solution.py:417
  18.9 4.2 %collective-permute-start.6 = (bf16[24,64,256]{2,1,0:T(8,128)(2,1)S(1)}, bf16[24,64,256]{2,1,0:T(8,128)(2,1)S(1)}, u32[]{:S(2)}, u32[]{:S(2)}) collective-permute-start(bf16[24,64,256]{2,1,0:T(8,128)(2,1)S(1)} %constant_dynamic-update-slice_fusion.refs_1_), channel_id=1, source_target_pairs={{0,4},{4,0},{8,12},{12,8},{16,20},{20,16},{24,28},{28,24},{1,5},{5... | collective-permute-start | bytes 2359304 | tf_op jit(solution)/shard_map/ppermute | solution.py:402
  19.0 2.6 %collective-permute-start.5 = (bf16[8,64,256]{2,1,0:T(8,128)(2,1)S(1)}, bf16[8,64,256]{2,1,0:T(8,128)(2,1)S(1)}, u32[]{:S(2)}, u32[]{:S(2)}) collective-permute-start(bf16[8,64,256]{2,1,0:T(8,128)(2,1)S(1)} %copy-done.1), channel_id=1, source_target_pairs={{0,4},{4,0},{8,12},{12,8},{16,20},{20,16},{24,28},{28,24},{1,5},{5... | collective-permute-start | bytes 786440 | tf_op jit(solution)/shard_map/ppermute | solution.py:402
  19.5 13.6 %collective-permute-start.7 = (bf16[8,64,256]{2,1,0:T(8,128)(2,1)S(1)}, bf16[8,64,256]{2,1,0:T(8,128)(2,1)S(1)}, u32[]{:S(2)}, u32[]{:S(2)}) collective-permute-start(bf16[8,64,256]{2,1,0:T(8,128)(2,1)S(1)} %collective-permute-done.2.refs_0_), channel_id=1, source_target_pairs={{0,8},{4,12},{8,0},{12,4},{16,24},{20,28},{24,16},{28,20},{1,9},{5... | collective-permute-start | bytes 786440 | tf_op jit(solution)/shard_map/ppermute | solution.py:402
  20.0 13.0 %collective-permute-start.8 = (bf16[8,64,256]{2,1,0:T(8,128)(2,1)S(1)}, bf16[8,64,256]{2,1,0:T(8,128)(2,1)S(1)}, u32[]{:S(2)}, u32[]{:S(2)}) collective-permute-start(bf16[8,64,256]{2,1,0:T(8,128)(2,1)S(1)} %collective-permute-done.2.refs_0_), channel_id=1, source_target_pairs={{0,16},{4,20},{8,24},{12,28},{16,0},{20,4},{24,8},{28,12},{1,17},{... | collective-permute-start | bytes 786440 | tf_op jit(solution)/shard_map/ppermute | solution.py:402
  21.6 12.7 %collective-permute-start.9 = (bf16[8,64,256]{2,1,0:T(8,128)(2,1)S(1)}, bf16[8,64,256]{2,1,0:T(8,128)(2,1)S(1)}, u32[]{:S(2)}, u32[]{:S(2)}) collective-permute-start(bf16[8,64,256]{2,1,0:T(8,128)(2,1)S(1)} %collective-permute-done.2.refs_0_), channel_id=1, source_target_pairs={{0,24},{4,28},{8,16},{12,20},{16,8},{20,12},{24,0},{28,4},{1,25},{... | collective-permute-start | bytes 786440 | tf_op jit(solution)/shard_map/ppermute | solution.py:402
  33.0 15.5 %copy-start.2 = (s32[1,256]{1,0:T(1,128)S(1)}, s32[1,256]{1,0:T(1,128)}, u32[]{:S(2)}) copy-start(s32[1,256]{1,0:T(1,128)} %slot_ref.1) | copy-start | bytes 3076
  34.4 2.2 %collective-permute-start.11 = (bf16[8,64,256]{2,1,0:T(8,128)(2,1)S(1)}, bf16[8,64,256]{2,1,0:T(8,128)(2,1)S(1)}, u32[]{:S(2)}, u32[]{:S(2)}) collective-permute-start(bf16[8,64,256]{2,1,0:T(8,128)(2,1)S(1)} %collective-permute-done.2.refs_0_), channel_id=1, source_target_pairs={{0,4},{4,0},{8,12},{12,8},{16,20},{20,16},{24,28},{28,24},{1,5},{5... | collective-permute-start | bytes 786440 | tf_op jit(solution)/shard_map/ppermute | solution.py:402
  34.4 2.9 %collective-permute-start.12 = (bf16[8,64,256]{2,1,0:T(8,128)(2,1)S(1)}, bf16[8,64,256]{2,1,0:T(8,128)(2,1)S(1)}, u32[]{:S(2)}, u32[]{:S(2)}) collective-permute-start(bf16[8,64,256]{2,1,0:T(8,128)(2,1)S(1)} %collective-permute-done.7.refs_1_), channel_id=1, source_target_pairs={{0,4},{4,0},{8,12},{12,8},{16,20},{20,16},{24,28},{28,24},{1,5},{5... | collective-permute-start | bytes 786440 | tf_op jit(solution)/shard_map/ppermute | solution.py:402
  34.9 2.4 %collective-permute-start.13 = (bf16[8,64,256]{2,1,0:T(8,128)(2,1)S(1)}, bf16[8,64,256]{2,1,0:T(8,128)(2,1)S(1)}, u32[]{:S(2)}, u32[]{:S(2)}) collective-permute-start(bf16[8,64,256]{2,1,0:T(8,128)(2,1)S(1)} %collective-permute-done.8.refs_2_), channel_id=1, source_target_pairs={{0,4},{4,0},{8,12},{12,8},{16,20},{20,16},{24,28},{28,24},{1,5},{5... | collective-permute-start | bytes 786440 | tf_op jit(solution)/shard_map/ppermute | solution.py:402
  34.9 2.4 %collective-permute-start.14 = (bf16[8,64,256]{2,1,0:T(8,128)(2,1)S(1)}, bf16[8,64,256]{2,1,0:T(8,128)(2,1)S(1)}, u32[]{:S(2)}, u32[]{:S(2)}) collective-permute-start(bf16[8,64,256]{2,1,0:T(8,128)(2,1)S(1)} %collective-permute-done.9.refs_3_), channel_id=1, source_target_pairs={{0,4},{4,0},{8,12},{12,8},{16,20},{20,16},{24,28},{28,24},{1,5},{5... | collective-permute-start | bytes 786440 | tf_op jit(solution)/shard_map/ppermute | solution.py:402
  35.4 15.8 %collective-permute-start.15 = (bf16[2064,128]{1,0:T(8,128)(2,1)S(1)}, bf16[2064,128]{1,0:T(8,128)(2,1)S(1)}, u32[]{:S(2)}, u32[]{:S(2)}) collective-permute-start(bf16[2064,128]{1,0:T(8,128)(2,1)S(1)} %get-tuple-element.32), channel_id=1, source_target_pairs={{0,1},{3,2},{1,3},{2,0},{4,5},{7,6},{5,7},{6,4},{8,9},{11,10},{9,1... | collective-permute-start | bytes 1585160 | tf_op jit(solution)/shard_map/ppermute | solution.py:438
  36.6 17.4 %collective-permute-start.16 = (bf16[2064,128]{1,0:T(8,128)(2,1)S(1)}, bf16[2064,128]{1,0:T(8,128)(2,1)S(1)}, u32[]{:S(2)}, u32[]{:S(2)}) collective-permute-start(bf16[2064,128]{1,0:T(8,128)(2,1)S(1)} %get-tuple-element.33), channel_id=1, source_target_pairs={{1,2},{2,1},{5,6},{6,5},{9,10},{10,9},{13,14},{14,13},{17,18},{18,... | collective-permute-start | bytes 1585160 | tf_op jit(solution)/shard_map/ppermute | solution.py:439
  47.2 16.1 %collective-permute-start.17 = (bf16[2064,128]{1,0:T(8,128)(2,1)S(1)}, bf16[2064,128]{1,0:T(8,128)(2,1)S(1)}, u32[]{:S(2)}, u32[]{:S(2)}) collective-permute-start(bf16[2064,128]{1,0:T(8,128)(2,1)S(1)} %get-tuple-element.34), channel_id=1, source_target_pairs={{1,0},{2,3},{5,4},{6,7},{9,8},{10,11},{13,12},{14,15},{17,16},{18,... | collective-permute-start | bytes 1585160 | tf_op jit(solution)/shard_map/ppermute | solution.py:444
  48.5 5.4 %collective-permute-start = (s32[1,256]{1,0:T(1,128)S(1)}, s32[1,256]{1,0:T(1,128)S(1)}, u32[]{:S(2)}, u32[]{:S(2)}) collective-permute-start(s32[1,256]{1,0:T(1,128)S(1)} %copy-done.2), channel_id=1, source_target_pairs={{0,3},{1,2},{2,1},{3,0},{4,7},{5,6},{6,5},{7,4},{8,11},{9,10},{10,... | collective-permute-start | bytes 3080 | tf_op jit(solution)/shard_map/ppermute | solution.py:402

commit v4 on v0

--- a/solution.py
+++ b/solution.py
@@ -13,7 +13,7 @@
 AHEAD = 2
 NAME_ROWS = 16
 PART = 256
-PARTS = 2
+PARTS = 1
 
 
 def log2(n):
@@ -69,10 +69,10 @@
         copies.append(pltpu.make_async_copy(rows_in.at[part], a_ref.at[part], sems.at[len(copies)]))
     at = 0
     for piece in pieces:
-        for n in range(0, piece.shape[0], rf):
-            part, whole = piece.at[pl.ds(n, rf)], panel.at[pl.ds(at, rf)]
+        for n in range(0, piece.shape[0], rf // 2):
+            part, whole = piece.at[pl.ds(n, rf // 2)], panel.at[pl.ds(at, rf // 2)]
             copies.append(pltpu.make_async_copy(part, whole, sems.at[len(copies)]))
-            at += rf
+            at += rf // 2
     for copy in copies:
         copy.start()
     copies.pop(0).wait()
@@ -241,7 +241,7 @@
                 pltpu.VMEM((rf, LANES), jnp.int32),
                 pltpu.SMEM((rf, n_places), jnp.int32),
                 pltpu.SMEM((rf, LANES), jnp.int32),
-                pltpu.SemaphoreType.DMA((3 + rf // PARTS + rows // rf,)),
+                pltpu.SemaphoreType.DMA((3 + rf // PARTS + 2 * rows // rf,)),
             ],
         ),
         compiler_params=pltpu.CompilerParams(
@@ -396,7 +396,7 @@
                 pltpu.VMEM((OSLOT, sub * LANES), jnp.float32),
                 pltpu.VMEM(names, jnp.int32),
                 pltpu.SMEM(names, jnp.int32),
-                pltpu.SemaphoreType.DMA((2 + 3 * 4,)),
+                pltpu.SemaphoreType.DMA((2 + 3 * 8,)),
             ],
         ),
         compiler_params=pltpu.CompilerParams(

time: 67.5 us -> 74.3 us (1.10)
  Pallas kernels: 28 us -> 35.9 us
  starting transfers between devices: 17.4 us -> 16.3 us
    pallas_call x2, Pallas kernels: 19.8 us -> 27.7 us  [partial_sums(): pl.pallas_call(functools.partial(partial_kernel, len(pieces), spans, cap,...]
    ppermute x1, waiting for transfers between devices: 10.3 us -> 13.3 us  [body(): from_c = lax.ppermute(to_c, 'grp', [(1, 0), (2, 3)])]
    ppermute x1, waiting for transfers between devices: 2.64 us -> 0.01 us  [body(): from_a = lax.ppermute(to_a, 'grp', [(0, 1), (3, 2), (1, 3), (2, 0)])]
    ppermute x1, starting transfers between devices: 1.2 us -> 0.01 us  [body(): from_a = lax.ppermute(to_a, 'grp', [(0, 1), (3, 2), (1, 3), (2, 0)])]
  transfers between devices with their start and end apart: 17 -> 17, of which waited for: 6 -> 6; matrix products, arithmetic and copies ran while one was open for 0% -> 0% of each run, Pallas kernels for 36% -> 43%
where the time goes in v4:
time: 74.3 us; the launch traced here: 74.1 us
  Pallas kernels  35.9 us (48%)
  waiting for transfers between devices  21.8 us (29%)
  starting transfers between devices  16.3 us (22%)
    pallas_call x2, Pallas kernels, partial_sums(): pl.pallas_call(functools.partial(partial_kernel, len(pieces), spans, cap,...  27.7 us
    ppermute x1, waiting for transfers between devices, body(): from_c = lax.ppermute(to_c, 'grp', [(1, 0), (2, 3)])  13.3 us
    ppermute x12, starting transfers between devices, swap(): lax.ppermute(x, axis, [(i, i ^ d) for i in range(lax.axis_size(axis))])  10.1 us
    ppermute x12, waiting for transfers between devices, swap(): lax.ppermute(x, axis, [(i, i ^ d) for i in range(lax.axis_size(axis))])  8.22 us
    ppermute x2, starting transfers between devices, take(): return lax.ppermute(x, 'grp', takes)  4.17 us
    pallas_call x1, Pallas kernels, owner_sums(): pl.pallas_call(last_kernel, out_shape=jax.ShapeDtypeStruct((OSLOT, sub *...  4.08 us
    pallas_call x1, Pallas kernels, with_numbers(): pl.pallas_call(numbers_kernel, out_shape=jax.ShapeDtypeStruct((rf * tile...  2.3 us
    pallas_call x1, Pallas kernels, owner_sums(): pl.pallas_call(early_kernel, out_shape=table, grid_spec=pl.GridSpec(grid=...  1.82 us
  transfers between devices with their start and end apart: 17, of which 6 were waited for; matrix products, arithmetic and copies ran while one was open for 0% of the time, Pallas kernels for 43%

profile of v4, /device:TPU:0, one launch (start us, length us, event | category | flops | bytes accessed | tf_op | source)
XLA Modules:
  0.0 74.1 jit_solution(9142677935049269263)
XLA Ops:
  0.0 0.0 copy-start.1
  0.0 2.9 %collective-permute-start = (bf16[8,64,256]{2,1,0:T(8,128)(2,1)}, bf16[8,64,256]{2,1,0:T(8,128)(2,1)S(1)}, u32[]{:S(2)}, u32[]{:S(2)}) collective-permute-start(bf16[8,64,256]{2,1,0:T(8,128)(2,1)} %refs_0_.1), channel_id=1, source_target_pairs={{0,8},{4,12},{8,0},{12,4},{16,24},{20,28},{24,16},{28,20},{1,9},{5... | collective-permute-start | bytes 786440 | tf_op jit(solution)/shard_map/ppermute | solution.py:410
  2.9 2.6 %collective-permute-start.1 = (bf16[8,64,256]{2,1,0:T(8,128)(2,1)}, bf16[8,64,256]{2,1,0:T(8,128)(2,1)S(1)}, u32[]{:S(2)}, u32[]{:S(2)}) collective-permute-start(bf16[8,64,256]{2,1,0:T(8,128)(2,1)} %refs_0_.1), channel_id=1, source_target_pairs={{1,0},{3,1},{0,2},{2,3},{5,4},{7,5},{4,6},{6,7},{9,8},{11,9},{8,10... | collective-permute-start | bytes 786440 | tf_op jit(solution)/shard_map/ppermute | solution.py:425
  5.5 1.5 %collective-permute-start.2 = (bf16[8,64,256]{2,1,0:T(8,128)(2,1)}, bf16[8,64,256]{2,1,0:T(8,128)(2,1)S(1)}, u32[]{:S(2)}, u32[]{:S(2)}) collective-permute-start(bf16[8,64,256]{2,1,0:T(8,128)(2,1)} %refs_0_.1), channel_id=1, source_target_pairs={{0,16},{4,20},{8,24},{12,28},{16,0},{20,4},{24,8},{28,12},{1,17},{... | collective-permute-start | bytes 786440 | tf_op jit(solution)/shard_map/ppermute | solution.py:410
  7.1 0.5 collective-permute-start.3
  7.5 2.3 %with_numbers.1.rows_in = bf16[528,1024]{1,0:T(8,128)(2,1)} custom-call(bf16[8,64,1024]{2,1,0:T(8,128)(2,1)} %a_ref.1, s32[8,256]{1,0:T(8,128)} %route_ref.1, s32[1,256]{1,0:T(1,128)} %slot_ref.1, s32[8,16]{1,0:T(8,128)} %cols_ref.1), custom_call_target="tpu_custom_call" | custom-call | flops 1 | bytes 1 | tf_op jit(solution)/shard_map/with_numbers/pallas_call | solution.py:41
  9.8 0.0 copy-start
  9.8 1.6 %collective-permute-start.9 = (bf16[528,1024]{1,0:T(8,128)(2,1)}, bf16[528,1024]{1,0:T(8,128)(2,1)S(1)}, u32[]{:S(2)}, u32[]{:S(2)}) collective-permute-start(bf16[528,1024]{1,0:T(8,128)(2,1)} %with_numbers.1.rows_in), channel_id=1, source_target_pairs={{1,0},{3,1},{0,2},{2,3},{5,4},{7,5},{4,6},{6,7},{9,8},{11,9},{8,10... | collective-permute-start | bytes 3244040 | tf_op jit(solution)/shard_map/ppermute | solution.py:425
  11.4 0.0 collective-permute-done
  11.4 0.2 collective-permute-done.1.refs_0_
  11.7 7.2 %collective-permute-done.2 = bf16[8,64,256]{2,1,0:T(8,128)(2,1)S(1)} collective-permute-done((bf16[8,64,256]{2,1,0:T(8,128)(2,1)}, bf16[8,64,256]{2,1,0:T(8,128)(2,1)S(1)}, u32[]{:S(2)}, u32[]{:S(2)}) %collective-permute-start.2) | collective-permute-done | bytes 262176 | tf_op jit(solution)/shard_map/ppermute | solution.py:410
  18.9 0.0 collective-permute-done.3
  18.9 0.1 collective-permute-start.5
  19.0 0.0 copy-done.1
  19.0 0.5 collective-permute-start.4
  19.5 0.5 collective-permute-start.6
  20.0 1.5 %collective-permute-start.7 = (bf16[8,64,256]{2,1,0:T(8,128)(2,1)S(1)}, bf16[8,64,256]{2,1,0:T(8,128)(2,1)S(1)}, u32[]{:S(2)}, u32[]{:S(2)}) collective-permute-start(bf16[8,64,256]{2,1,0:T(8,128)(2,1)S(1)} %collective-permute-done.1.refs_0_), channel_id=1, source_target_pairs={{0,16},{4,20},{8,24},{12,28},{16,0},{20,4},{24,8},{28,12},{1,17},{... | collective-permute-start | bytes 786440 | tf_op jit(solution)/shard_map/ppermute | solution.py:410
  21.5 0.1 collective-permute-done.4.refs_2_
  21.6 1.5 %collective-permute-start.8 = (bf16[8,64,256]{2,1,0:T(8,128)(2,1)S(1)}, bf16[8,64,256]{2,1,0:T(8,128)(2,1)S(1)}, u32[]{:S(2)}, u32[]{:S(2)}) collective-permute-start(bf16[8,64,256]{2,1,0:T(8,128)(2,1)S(1)} %collective-permute-done.1.refs_0_), channel_id=1, source_target_pairs={{0,24},{4,28},{8,16},{12,20},{16,8},{20,12},{24,0},{28,4},{1,25},{... | collective-permute-start | bytes 786440 | tf_op jit(solution)/shard_map/ppermute | solution.py:410
  23.1 0.0 collective-permute-done.5.refs_3_
  23.1 0.0 copy-done
  23.1 13.9 %partial_sums.2 = (bf16[2064,128]{1,0:T(8,128)(2,1)S(1)}, bf16[2064,128]{1,0:T(8,128)(2,1)S(1)}, bf16[2064,128]{1,0:T(8,128)(2,1)S(1)}) custom-call(bf16[528,1024]{1,0:T(8,128)(2,1)S(1)} %copy-done, bf16[8,64,256]{2,1,0:T(8,128)(2,1)S(1)} %copy-done.1, bf16[24,64,256]{2,1,0:T(8,128)(2,1)S(1)} %constant_dynamic-update-slice_fusion.refs_1_, ...), custom_call_target="tpu_custom_call" | custom-call | flops 1 | bytes 1 | tf_op jit(solution)/shard_map/partial_sums/pallas_call | solution.py:225
  37.0 0.0 collective-permute-done.6.refs_1_
  37.0 0.0 collective-permute-done.7.refs_2_
  37.0 0.0 collective-permute-done.8.refs_3_
  37.1 0.1 collective-permute-start.10
  37.1 0.5 collective-permute-start.11
  37.6 0.1 collective-permute-start.12
  37.7 0.4 collective-permute-start.13
  38.1 0.0 collective-permute-done.9.rows_in
  38.2 0.0 collective-permute-start.14
  38.2 0.5 collective-permute-done.10.refs_4_
  38.7 0.7 collective-permute-start.15
  39.4 0.0 collective-permute-done.11.refs_5_
  39.4 0.0 collective-permute-done.12.refs_6_
  39.4 0.4 collective-permute-done.13.refs_7_
  39.8 13.8 %partial_sums.3 = (bf16[2064,128]{1,0:T(8,128)(2,1)S(1)}, bf16[2064,128]{1,0:T(8,128)(2,1)S(1)}) custom-call(bf16[528,1024]{1,0:T(8,128)(2,1)S(1)} %collective-permute-done.9.rows_in, bf16[8,64,256]{2,1,0:T(8,128)(2,1)S(1)} %collective-permute-done.1.refs_0_, bf16[8,64,256]{2,1,0:T(8,128)(2,1)S(1)} %collective-permute-done.6.refs_1_, ...), custom_call_target="tpu_custom_call" | custom-call | flops 1 | bytes 1 | tf_op jit(solution)/shard_map/partial_sums/pallas_call | solution.py:225
  53.6 1.3 %collective-permute-start.16 = (bf16[2064,128]{1,0:T(8,128)(2,1)S(1)}, bf16[2064,128]{1,0:T(8,128)(2,1)S(1)}, u32[]{:S(2)}, u32[]{:S(2)}) collective-permute-start(bf16[2064,128]{1,0:T(8,128)(2,1)S(1)} %get-tuple-element.34), channel_id=1, source_target_pairs={{1,0},{2,3},{5,4},{6,7},{9,8},{10,11},{13,12},{14,15},{17,16},{18,... | collective-permute-start | bytes 1585160 | tf_op jit(solution)/shard_map/ppermute | solution.py:452
  54.9 0.0 collective-permute-done.14.refs_2_
  54.9 1.8 %early_sums.1.table = f32[128,32,128]{2,1,0:T(8,128)S(1)} custom-call(bf16[2064,128]{1,0:T(8,128)(2,1)S(1)} %get-tuple-element.23.refs_0_, bf16[2064,128]{1,0:T(8,128)(2,1)S(1)} %get-tuple-element.31.refs_1_, bf16[2064,128]{1,0:T(8,128)(2,1)S(1)} %collective-permute-done.14.refs_2_), custom_call_target="tpu_custom_call" | custom-call | tf_op jit(solution)/shard_map/early_sums/pallas_call | solution.py:367
  56.7 0.0 collective-permute-done.15.from_b
  56.7 13.3 %collective-permute-done.16.from_c = bf16[2064,128]{1,0:T(8,128)(2,1)S(1)} collective-permute-done((bf16[2064,128]{1,0:T(8,128)(2,1)S(1)}, bf16[2064,128]{1,0:T(8,128)(2,1)S(1)}, u32[]{:S(2)}, u32[]{:S(2)}) %collective-permute-start.16) | collective-permute-done | bytes 528416 | tf_op jit(solution)/shard_map/ppermute | solution.py:452
  70.0 4.1 %owner_sums.1 = f32[128,4096]{1,0:T(8,128)} custom-call(f32[128,32,128]{2,1,0:T(8,128)S(1)} %early_sums.1.table, bf16[2064,128]{1,0:T(8,128)(2,1)S(1)} %collective-permute-done.15.from_b, bf16[2064,128]{1,0:T(8,128)(2,1)S(1)} %collective-permute-done.16.from_c), custom_call_target="tpu_custom_call" | custom-call | tf_op jit(solution)/shard_map/owner_sums/pallas_call | solution.py:386
  (3 shorter events, 0.1 us)
Async XLA Ops:
  0.0 19.0 %copy-start.1 = (bf16[8,64,256]{2,1,0:T(8,128)(2,1)S(1)}, bf16[8,64,256]{2,1,0:T(8,128)(2,1)}, u32[]{:S(2)}) copy-start(bf16[8,64,256]{2,1,0:T(8,128)(2,1)} %refs_0_.1) | copy-start | bytes 786436
  0.0 11.4 %collective-permute-start = (bf16[8,64,256]{2,1,0:T(8,128)(2,1)}, bf16[8,64,256]{2,1,0:T(8,128)(2,1)S(1)}, u32[]{:S(2)}, u32[]{:S(2)}) collective-permute-start(bf16[8,64,256]{2,1,0:T(8,128)(2,1)} %refs_0_.1), channel_id=1, source_target_pairs={{0,8},{4,12},{8,0},{12,4},{16,24},{20,28},{24,16},{28,20},{1,9},{5... | collective-permute-start | bytes 786440 | tf_op jit(solution)/shard_map/ppermute | solution.py:410
  2.9 8.7 %collective-permute-start.1 = (bf16[8,64,256]{2,1,0:T(8,128)(2,1)}, bf16[8,64,256]{2,1,0:T(8,128)(2,1)S(1)}, u32[]{:S(2)}, u32[]{:S(2)}) collective-permute-start(bf16[8,64,256]{2,1,0:T(8,128)(2,1)} %refs_0_.1), channel_id=1, source_target_pairs={{1,0},{3,1},{0,2},{2,3},{5,4},{7,5},{4,6},{6,7},{9,8},{11,9},{8,10... | collective-permute-start | bytes 786440 | tf_op jit(solution)/shard_map/ppermute | solution.py:425
  5.5 13.3 %collective-permute-start.2 = (bf16[8,64,256]{2,1,0:T(8,128)(2,1)}, bf16[8,64,256]{2,1,0:T(8,128)(2,1)S(1)}, u32[]{:S(2)}, u32[]{:S(2)}) collective-permute-start(bf16[8,64,256]{2,1,0:T(8,128)(2,1)} %refs_0_.1), channel_id=1, source_target_pairs={{0,16},{4,20},{8,24},{12,28},{16,0},{20,4},{24,8},{28,12},{1,17},{... | collective-permute-start | bytes 786440 | tf_op jit(solution)/shard_map/ppermute | solution.py:410
  7.1 11.8 %collective-permute-start.3 = (bf16[8,64,256]{2,1,0:T(8,128)(2,1)}, bf16[8,64,256]{2,1,0:T(8,128)(2,1)S(1)}, u32[]{:S(2)}, u32[]{:S(2)}) collective-permute-start(bf16[8,64,256]{2,1,0:T(8,128)(2,1)} %refs_0_.1), channel_id=1, source_target_pairs={{0,24},{4,28},{8,16},{12,20},{16,8},{20,12},{24,0},{28,4},{1,25},{... | collective-permute-start | bytes 786440 | tf_op jit(solution)/shard_map/ppermute | solution.py:410
  9.8 13.3 %copy-start = (bf16[528,1024]{1,0:T(8,128)(2,1)S(1)}, bf16[528,1024]{1,0:T(8,128)(2,1)}, u32[]{:S(2)}) copy-start(bf16[528,1024]{1,0:T(8,128)(2,1)} %with_numbers.1.rows_in) | copy-start | bytes 3244036
  9.8 28.3 %collective-permute-start.9 = (bf16[528,1024]{1,0:T(8,128)(2,1)}, bf16[528,1024]{1,0:T(8,128)(2,1)S(1)}, u32[]{:S(2)}, u32[]{:S(2)}) collective-permute-start(bf16[528,1024]{1,0:T(8,128)(2,1)} %with_numbers.1.rows_in), channel_id=1, source_target_pairs={{1,0},{3,1},{0,2},{2,3},{5,4},{7,5},{4,6},{6,7},{9,8},{11,9},{8,10... | collective-permute-start | bytes 3244040 | tf_op jit(solution)/shard_map/ppermute | solution.py:425
  18.9 4.2 %collective-permute-start.5 = (bf16[24,64,256]{2,1,0:T(8,128)(2,1)S(1)}, bf16[24,64,256]{2,1,0:T(8,128)(2,1)S(1)}, u32[]{:S(2)}, u32[]{:S(2)}) collective-permute-start(bf16[24,64,256]{2,1,0:T(8,128)(2,1)S(1)} %constant_dynamic-update-slice_fusion.refs_1_), channel_id=1, source_target_pairs={{0,4},{4,0},{8,12},{12,8},{16,20},{20,16},{24,28},{28,24},{1,5},{5... | collective-permute-start | bytes 2359304 | tf_op jit(solution)/shard_map/ppermute | solution.py:410
  19.0 2.6 %collective-permute-start.4 = (bf16[8,64,256]{2,1,0:T(8,128)(2,1)S(1)}, bf16[8,64,256]{2,1,0:T(8,128)(2,1)S(1)}, u32[]{:S(2)}, u32[]{:S(2)}) collective-permute-start(bf16[8,64,256]{2,1,0:T(8,128)(2,1)S(1)} %copy-done.1), channel_id=1, source_target_pairs={{0,4},{4,0},{8,12},{12,8},{16,20},{20,16},{24,28},{28,24},{1,5},{5... | collective-permute-start | bytes 786440 | tf_op jit(solution)/shard_map/ppermute | solution.py:410
  19.5 17.5 %collective-permute-start.6 = (bf16[8,64,256]{2,1,0:T(8,128)(2,1)S(1)}, bf16[8,64,256]{2,1,0:T(8,128)(2,1)S(1)}, u32[]{:S(2)}, u32[]{:S(2)}) collective-permute-start(bf16[8,64,256]{2,1,0:T(8,128)(2,1)S(1)} %collective-permute-done.1.refs_0_), channel_id=1, source_target_pairs={{0,8},{4,12},{8,0},{12,4},{16,24},{20,28},{24,16},{28,20},{1,9},{5... | collective-permute-start | bytes 786440 | tf_op jit(solution)/shard_map/ppermute | solution.py:410
  20.0 17.0 %collective-permute-start.7 = (bf16[8,64,256]{2,1,0:T(8,128)(2,1)S(1)}, bf16[8,64,256]{2,1,0:T(8,128)(2,1)S(1)}, u32[]{:S(2)}, u32[]{:S(2)}) collective-permute-start(bf16[8,64,256]{2,1,0:T(8,128)(2,1)S(1)} %collective-permute-done.1.refs_0_), channel_id=1, source_target_pairs={{0,16},{4,20},{8,24},{12,28},{16,0},{20,4},{24,8},{28,12},{1,17},{... | collective-permute-start | bytes 786440 | tf_op jit(solution)/shard_map/ppermute | solution.py:410
  21.6 15.4 %collective-permute-start.8 = (bf16[8,64,256]{2,1,0:T(8,128)(2,1)S(1)}, bf16[8,64,256]{2,1,0:T(8,128)(2,1)S(1)}, u32[]{:S(2)}, u32[]{:S(2)}) collective-permute-start(bf16[8,64,256]{2,1,0:T(8,128)(2,1)S(1)} %collective-permute-done.1.refs_0_), channel_id=1, source_target_pairs={{0,24},{4,28},{8,16},{12,20},{16,8},{20,12},{24,0},{28,4},{1,25},{... | collective-permute-start | bytes 786440 | tf_op jit(solution)/shard_map/ppermute | solution.py:410
  37.1 1.6 %collective-permute-start.10 = (bf16[8,64,256]{2,1,0:T(8,128)(2,1)S(1)}, bf16[8,64,256]{2,1,0:T(8,128)(2,1)S(1)}, u32[]{:S(2)}, u32[]{:S(2)}) collective-permute-start(bf16[8,64,256]{2,1,0:T(8,128)(2,1)S(1)} %collective-permute-done.1.refs_0_), channel_id=1, source_target_pairs={{0,4},{4,0},{8,12},{12,8},{16,20},{20,16},{24,28},{28,24},{1,5},{5... | collective-permute-start | bytes 786440 | tf_op jit(solution)/shard_map/ppermute | solution.py:410
  37.1 2.2 %collective-permute-start.11 = (bf16[8,64,256]{2,1,0:T(8,128)(2,1)S(1)}, bf16[8,64,256]{2,1,0:T(8,128)(2,1)S(1)}, u32[]{:S(2)}, u32[]{:S(2)}) collective-permute-start(bf16[8,64,256]{2,1,0:T(8,128)(2,1)S(1)} %collective-permute-done.6.refs_1_), channel_id=1, source_target_pairs={{0,4},{4,0},{8,12},{12,8},{16,20},{20,16},{24,28},{28,24},{1,5},{5... | collective-permute-start | bytes 786440 | tf_op jit(solution)/shard_map/ppermute | solution.py:410
  37.6 1.8 %collective-permute-start.12 = (bf16[8,64,256]{2,1,0:T(8,128)(2,1)S(1)}, bf16[8,64,256]{2,1,0:T(8,128)(2,1)S(1)}, u32[]{:S(2)}, u32[]{:S(2)}) collective-permute-start(bf16[8,64,256]{2,1,0:T(8,128)(2,1)S(1)} %collective-permute-done.7.refs_2_), channel_id=1, source_target_pairs={{0,4},{4,0},{8,12},{12,8},{16,20},{20,16},{24,28},{28,24},{1,5},{5... | collective-permute-start | bytes 786440 | tf_op jit(solution)/shard_map/ppermute | solution.py:410
  37.7 2.1 %collective-permute-start.13 = (bf16[8,64,256]{2,1,0:T(8,128)(2,1)S(1)}, bf16[8,64,256]{2,1,0:T(8,128)(2,1)S(1)}, u32[]{:S(2)}, u32[]{:S(2)}) collective-permute-start(bf16[8,64,256]{2,1,0:T(8,128)(2,1)S(1)} %collective-permute-done.8.refs_3_), channel_id=1, source_target_pairs={{0,4},{4,0},{8,12},{12,8},{16,20},{20,16},{24,28},{28,24},{1,5},{5... | collective-permute-start | bytes 786440 | tf_op jit(solution)/shard_map/ppermute | solution.py:410
  38.2 16.7 %collective-permute-start.14 = (bf16[2064,128]{1,0:T(8,128)(2,1)S(1)}, bf16[2064,128]{1,0:T(8,128)(2,1)S(1)}, u32[]{:S(2)}, u32[]{:S(2)}) collective-permute-start(bf16[2064,128]{1,0:T(8,128)(2,1)S(1)} %get-tuple-element.32), channel_id=1, source_target_pairs={{0,1},{3,2},{1,3},{2,0},{4,5},{7,6},{5,7},{6,4},{8,9},{11,10},{9,1... | collective-permute-start | bytes 1585160 | tf_op jit(solution)/shard_map/ppermute | solution.py:446
  38.7 18.0 %collective-permute-start.15 = (bf16[2064,128]{1,0:T(8,128)(2,1)S(1)}, bf16[2064,128]{1,0:T(8,128)(2,1)S(1)}, u32[]{:S(2)}, u32[]{:S(2)}) collective-permute-start(bf16[2064,128]{1,0:T(8,128)(2,1)S(1)} %get-tuple-element.33), channel_id=1, source_target_pairs={{1,2},{2,1},{5,6},{6,5},{9,10},{10,9},{13,14},{14,13},{17,18},{18,... | collective-permute-start | bytes 1585160 | tf_op jit(solution)/shard_map/ppermute | solution.py:447
  53.6 16.5 %collective-permute-start.16 = (bf16[2064,128]{1,0:T(8,128)(2,1)S(1)}, bf16[2064,128]{1,0:T(8,128)(2,1)S(1)}, u32[]{:S(2)}, u32[]{:S(2)}) collective-permute-start(bf16[2064,128]{1,0:T(8,128)(2,1)S(1)} %get-tuple-element.34), channel_id=1, source_target_pairs={{1,0},{2,3},{5,4},{6,7},{9,8},{10,11},{13,12},{14,15},{17,16},{18,... | collective-permute-start | bytes 1585160 | tf_op jit(solution)/shard_map/ppermute | solution.py:452
